TPU v7x, 128 devices: a whole 4x4x4 slice. The times are simulated.
128 devices in a mesh: gz: 128 (over z, y, x, core).
Axes of the slice: x: 4, y: 4, z: 4, core: 2. Of those that a mesh axis runs over, the one named last changes fastest.
Arguments:
- fraction: float32 [512, 256, 256], P('gz'), may hold values from 0 to 1
- column_dir: int32 [512, 256, 256], P('gz'), may hold values from 0 to 3
- divergence: float32 [512, 256, 256], P('gz'), may hold values from -6 to 6
Outputs:
- curvature: float32 [512, 256, 256], P('gz')
- pressure: float32 [512, 256, 256], P('gz')
Inputs may be any that keep to these rules, and one draw needn't show every extreme that they name: `column_dir`: 0 names a column along z, 1 along x, 2 along y, 3 a cell without interface.
All inputs are finite; a program needn't handle non-finite values.
Results may differ from a plain program's by a relative error of at most 0.00065.
Values sent between devices are 32-bit elements; how exact they have to be, the bound alone decides.
A program may use at most 128 MiB of HBM per device.

v0:
```python
import jax
import jax.numpy as jnp
from jax import lax
from jax.sharding import PartitionSpec as P

TENSION = 0.2
SHIFT_SCALE = 16.0


def padded(block, sides, width):
    for axis, dim in sides:
        count = lax.axis_size(axis)
        forward = [(i, i + 1) for i in range(count - 1)]
        backward = [(target, source) for source, target in forward]
        low = lax.ppermute(
            lax.slice_in_dim(block, block.shape[dim] - width, None, axis=dim), axis, forward
        )
        high = lax.ppermute(lax.slice_in_dim(block, 0, width, axis=dim), axis, backward)
        block = jnp.concatenate([low, block, high], axis=dim)
    return block


def from_behind(block, axis, distance):
    devices = range(lax.axis_size(axis))
    route = [(i - distance, i) for i in devices if i - distance in devices]
    return lax.ppermute(block, axis, route)


def curvature_family(heights):
    slope_a = 0.5 * (heights[1, 0] - heights[-1, 0])
    slope_b = 0.5 * (heights[0, 1] - heights[0, -1])
    bend_aa = heights[1, 0] - 2.0 * heights[0, 0] + heights[-1, 0]
    bend_bb = heights[0, 1] - 2.0 * heights[0, 0] + heights[0, -1]
    bend_ab = 0.25 * (heights[1, 1] - heights[1, -1] - heights[-1, 1] + heights[-1, -1])
    weight = 1.0 + slope_a * slope_a + slope_b * slope_b
    upper = (
        bend_aa * (1.0 + slope_b * slope_b)
        + bend_bb * (1.0 + slope_a * slope_a)
        - 2.0 * slope_a * slope_b * bend_ab
    )
    return upper / (weight * jnp.sqrt(weight))


def curvature_of(extended, column_dir):
    count = extended.shape[0] - 6
    offsets = (-1, 0, 1)
    along_z = extended[0:count]
    along_x = jnp.roll(extended, 3, 1)
    along_y = jnp.roll(extended, 3, 2)
    for step in range(1, 7):
        along_z = along_z + extended[step : step + count]
        along_x = along_x + jnp.roll(extended, 3 - step, 1)
        along_y = along_y + jnp.roll(extended, 3 - step, 2)
    family_z = {
        (first, second): jnp.roll(jnp.roll(along_z, -first, 1), -second, 2)
        for first in offsets
        for second in offsets
    }
    kappa_z = curvature_family(family_z)
    family_x = {
        (first, second): jnp.roll(along_x[3 + first : 3 + first + count], -second, 2)
        for first in offsets
        for second in offsets
    }
    kappa_x = curvature_family(family_x)
    family_y = {
        (first, second): jnp.roll(along_y[3 + first : 3 + first + count], -second, 1)
        for first in offsets
        for second in offsets
    }
    kappa_y = curvature_family(family_y)
    zero = jnp.zeros_like(kappa_z)
    return jnp.where(
        column_dir == 0,
        kappa_z,
        jnp.where(column_dir == 1, kappa_x, jnp.where(column_dir == 2, kappa_y, zero)),
    )


def tension_term(frac_pad, kappa_pad):
    face_up = 0.5 * (kappa_pad[1:-1] + kappa_pad[2:]) * (frac_pad[2:] - frac_pad[1:-1])
    face_down = 0.5 * (kappa_pad[:-2] + kappa_pad[1:-1]) * (frac_pad[1:-1] - frac_pad[:-2])
    kappa_mid = kappa_pad[1:-1]
    frac_mid = frac_pad[1:-1]
    total = face_up - face_down
    for axis in (1, 2):
        face_plus = (
            0.5
            * (kappa_mid + jnp.roll(kappa_mid, -1, axis))
            * (jnp.roll(frac_mid, -1, axis) - frac_mid)
        )
        total = total + face_plus - jnp.roll(face_plus, 1, axis)
    return TENSION * total


def mode_diagonal(size_x, size_y, wall_shift):
    waves_x = 2.0 * jnp.sin(jnp.pi * jnp.arange(size_x).astype(jnp.float32) / size_x)
    waves_y = 2.0 * jnp.sin(jnp.pi * jnp.arange(size_y).astype(jnp.float32) / size_y)
    diag = -(2.0 + (waves_x * waves_x)[:, None] + (waves_y * waves_y)[None, :] + wall_shift)
    return diag.reshape(size_x * size_y)


def thomas(rows, diag):
    start = jnp.zeros(rows.shape[1:], jnp.float32)

    def forward(carry, row):
        prev_c, prev_d = carry
        denom = diag - prev_c
        now_c = 1.0 / denom
        now_d = (row - prev_d) / denom
        return ((now_c, now_d), (now_c, now_d))

    final, sweeps = lax.scan(forward, (start, start), rows)

    def backward(above, item):
        coef, value = item
        result = value - coef * above
        return (result, result)

    final, solved = lax.scan(backward, start, sweeps, reverse=True)
    return solved


def cas_table(size):
    counter = jnp.arange(size, dtype=jnp.int32)
    phase = counter[:, None] * counter[None, :] % size
    angle = 2.0 * jnp.pi / size * phase.astype(jnp.float32)
    return jnp.cos(angle) + jnp.sin(angle)


def hartley_planes(field, table_x, table_y):
    inner = jnp.einsum("ai,kij->kaj", table_x, field, precision=lax.Precision.HIGHEST)
    return jnp.einsum("kaj,jb->kab", inner, table_y, precision=lax.Precision.HIGHEST)


def reduce_rows(own, below, above, diag_below, diag_above):
    coef_a, coef_b, coef_c, value = own
    scale_low = -coef_a / diag_below
    scale_up = -coef_c / diag_above
    new_a = scale_low * below[0]
    new_b = coef_b + scale_low * below[2] + scale_up * above[0]
    new_c = scale_up * above[2]
    new_d = value + scale_low * below[3] + scale_up * above[3]
    return (new_a, new_b, new_c, new_d)


def shards(fraction, column_dir, divergence):
    count, size_x, size_y = fraction.shape
    modes = size_x * size_y
    devices = lax.axis_size("gz")
    extended = padded(fraction, (("gz", 0),), 3)
    kappa = curvature_of(extended, column_dir)
    kappa_pad = padded(kappa, (("gz", 0),), 1)
    source = divergence + tension_term(extended[2:-2], kappa_pad)
    table_x = cas_table(size_x)
    table_y = cas_table(size_y)
    spectrum = hartley_planes(source, table_x, table_y).reshape(count, modes)
    planes_total = count * devices
    wall_shift = SHIFT_SCALE / float(planes_total * planes_total)
    diag = mode_diagonal(size_x, size_y, wall_shift)
    inner_rows = count - 1
    row_ids = jnp.arange(inner_rows, dtype=jnp.int32)[:, None]
    unit_low = jnp.where(row_ids == 0, -1.0, 0.0) * jnp.ones((1, modes), jnp.float32)
    unit_high = jnp.where(row_ids == inner_rows - 1, -1.0, 0.0) * jnp.ones((1, modes), jnp.float32)
    stacked = jnp.stack([spectrum[:-1], unit_low, unit_high], axis=1)
    solved = thomas(stacked, diag)
    base = solved[:, 0]
    low_reply = solved[:, 1]
    high_reply = solved[:, 2]
    near = low_reply[0]
    far = low_reply[-1]
    upper_first = from_behind(base[0], "gz", -1)
    reduced_rhs = spectrum[-1] - base[-1] - upper_first
    position = lax.axis_index("gz")
    beta = diag + 2.0 * near
    beta_top = diag + near
    rows = (
        jnp.where(position > 0, far, 0.0),
        jnp.where(position == devices - 1, beta_top, beta),
        jnp.where(position < devices - 1, far, 0.0),
        reduced_rhs,
    )
    for level in range(devices.bit_length()):
        step = 1 << level
        if step < devices:
            below = from_behind((rows[0], rows[1], rows[2], rows[3]), "gz", step)
            above = from_behind((rows[0], rows[1], rows[2], rows[3]), "gz", -step)
            diag_below = jnp.where(position >= step, below[1], 1.0)
            diag_above = jnp.where(position + step < devices, above[1], 1.0)
            rows = reduce_rows(rows, below, above, diag_below, diag_above)
    boundary = rows[3] / rows[1]
    lower_value = from_behind(boundary, "gz", 1)
    interior = base + lower_value[None, :] * low_reply + boundary[None, :] * high_reply
    modal = jnp.concatenate([interior, boundary[None, :]], axis=0).reshape(count, size_x, size_y)
    pressure = hartley_planes(modal, table_x, table_y) / (size_x * size_y)
    return (kappa, pressure)


def solution(mesh):
    return jax.shard_map(
        shards,
        mesh=mesh,
        in_specs=(P("gz", None, None), P("gz", None, None), P("gz", None, None)),
        out_specs=(P("gz", None, None), P("gz", None, None)),
        check_vma=False,
    )
```

profile of v0, /device:TPU:1, one launch (start us, length us, event | category | flops | bytes accessed | tf_op | source)
XLA Modules:
  0.0 463.3 jit_solution(11808498774528131720)
XLA Ops:
  3.1 4.5 collective-permute-start
  12.3 4.5 collective-permute-done
  46.5 8.2 %fusion.15 = f32[10,256,256]{2,1,0:T(8,128)S(1)} fusion(f32[10,256,256]{2,1,0:T(8,128)S(1)} %get-tuple-element.346, f32[10,256,253]{2,1,0:T(8,128)} %get-tuple-element.298, f32[10,256,3]{2,1,0:T(8,128)S(1)} %get-tuple-element.300, f32[10,256,254]{2,1,0:T(8,128)} %get-tuple-element.302, f32[10,256,2]{2,1,0:T(8,128)} %get-tuple-element.304, ...), kind=kLoop, calls=%fused_computation.35 | loop fusion | flops 7864320 | bytes 20971520 | tf_op jit(solution)/shard_map/add | solution.py:53
  61.9 11.3 %fusion.17 = f32[4,256,256]{2,1,0:T(8,128)S(1)} fusion(f32[4,256,1]{2,1,0:T(8,128)} %get-tuple-element.355, f32[4,256,255]{2,1,0:T(8,128)} %get-tuple-element.353, f32[4,256,255]{2,1,0:T(8,128)} %get-tuple-element.354, f32[4,256,1]{2,1,0:T(8,128)} %get-tuple-element.356, f32[4,256,1]{2,1,0:T(8,128)} %get-tuple-element.324, ...), kind=kLoop, calls=%fused_computation.43 | loop fusion | flops 27262976 | bytes 30408704 | tf_op jit(solution)/shard_map/jit(_where)/select_n | solution.py:73
  96.4 20.4 %while.34 = (s32[]{:T(128)}, f32[3,65536]{1,0:T(4,128)S(1)}, f32[3,65536]{1,0:T(4,128)}, f32[3,3,65536]{2,1,0:T(4,128)}, f32[3,3,65536]{2,1,0:T(4,128)}, /*index...) while((s32[]{:T(128)}, f32[3,65536]{1,0:T(4,128)S(1)}, ...), condition=%wide.region_1.2_spmd.clone, body=%wide.region_0.1_spmd.clone.sunk | while | flops 1376259 | bytes 9177715 | solution.py:113
  118.9 9.6 %while.35 = (s32[]{:T(128)}, f32[3,65536]{1,0:T(4,128)S(1)}, f32[3,3,65536]{2,1,0:T(4,128)}, f32[3,3,65536]{2,1,0:T(4,128)}, f32[3,3,65536]{2,1,0:T(4,128)}, /*index=5*/s32[]{:T(128)}, s32[]{:T(128)}, s32[]{:T(128)}) while((s32[]{:T(128)}, f32[3,65536]{1,0:T(4,128)S(1)}, f32[3,3,65536]{2,1,0:T(4,128)}, f32[3,3,65536]{2,1,0:T(4,128)}, ...), condition=%wide.region_3.4_spmd.clone, body=%wide.region_2.3_spmd.clone.sunk | while | flops 589828 | bytes 4718703 | solution.py:120
  165.9 10.0 %collective-permute-start.13 = (f32[65536]{0:T(1024)S(1)}, f32[65536]{0:T(1024)S(1)}, u32[]{:S(2)}, u32[]{:S(2)}) collective-permute-start(f32[65536]{0:T(1024)S(1)} %get-tuple-element.263), channel_id=1, source_target_pairs={{0,2},{1,3},{2,4},{3,5},{4,6},{5,7},{6,8},{7,9},{8,10},{9,11},{10,... | collective-permute-start | bytes 786440 | tf_op jit(solution)/shard_map/ppermute | solution.py:26
  179.3 9.5 %collective-permute-done.16 = f32[65536]{0:T(1024)} collective-permute-done((f32[65536]{0:T(1024)S(1)}, f32[65536]{0:T(1024)}, u32[]{:S(2)}, u32[]{:S(2)}) %collective-permute-start.16) | collective-permute-done | bytes 262176 | tf_op jit(solution)/shard_map/ppermute | solution.py:26
  189.8 5.4 %collective-permute-start.18 = (f32[65536]{0:T(1024)S(1)}, f32[65536]{0:T(1024)S(1)}, u32[]{:S(2)}, u32[]{:S(2)}) collective-permute-start(f32[65536]{0:T(1024)S(1)} %get-tuple-element.262), channel_id=1, source_target_pairs={{0,2},{1,3},{2,4},{3,5},{4,6},{5,7},{6,8},{7,9},{8,10},{9,11},{10,... | collective-permute-start | bytes 786440 | tf_op jit(solution)/shard_map/ppermute | solution.py:26
  196.5 4.8 %collective-permute-start.17 = (f32[65536]{0:T(1024)S(1)}, f32[65536]{0:T(1024)S(1)}, u32[]{:S(2)}, u32[]{:S(2)}) collective-permute-start(f32[65536]{0:T(1024)S(1)} %get-tuple-element.260), channel_id=1, source_target_pairs={{0,2},{1,3},{2,4},{3,5},{4,6},{5,7},{6,8},{7,9},{8,10},{9,11},{10,... | collective-permute-start | bytes 786440 | tf_op jit(solution)/shard_map/ppermute | solution.py:26
  202.6 7.6 %collective-permute-start.21 = (f32[65536]{0:T(1024)S(1)}, f32[65536]{0:T(1024)S(1)}, u32[]{:S(2)}, u32[]{:S(2)}) collective-permute-start(f32[65536]{0:T(1024)S(1)} %get-tuple-element.258), channel_id=1, source_target_pairs={{0,4},{1,5},{2,6},{3,7},{4,8},{5,9},{6,10},{7,11},{8,12},{9,13},{1... | collective-permute-start | bytes 786440 | tf_op jit(solution)/shard_map/ppermute | solution.py:26
  211.6 7.3 %collective-permute-start.20 = (f32[65536]{0:T(1024)S(1)}, f32[65536]{0:T(1024)S(1)}, u32[]{:S(2)}, u32[]{:S(2)}) collective-permute-start(f32[65536]{0:T(1024)S(1)} %multiply_add_fusion.8), channel_id=1, source_target_pairs={{0,4},{1,5},{2,6},{3,7},{4,8},{5,9},{6,10},{7,11},{8,12},{9,13},{1... | collective-permute-start | bytes 786440 | tf_op jit(solution)/shard_map/ppermute | solution.py:26
  224.1 11.3 %collective-permute-done.23 = f32[65536]{0:T(1024)} collective-permute-done((f32[65536]{0:T(1024)S(1)}, f32[65536]{0:T(1024)}, u32[]{:S(2)}, u32[]{:S(2)}) %collective-permute-start.23) | collective-permute-done | bytes 262176 | tf_op jit(solution)/shard_map/ppermute | solution.py:26
  239.6 8.4 %collective-permute-start.25 = (f32[65536]{0:T(1024)S(1)}, f32[65536]{0:T(1024)S(1)}, u32[]{:S(2)}, u32[]{:S(2)}) collective-permute-start(f32[65536]{0:T(1024)S(1)} %get-tuple-element.255), channel_id=1, source_target_pairs={{0,4},{1,5},{2,6},{3,7},{4,8},{5,9},{6,10},{7,11},{8,12},{9,13},{1... | collective-permute-start | bytes 786440 | tf_op jit(solution)/shard_map/ppermute | solution.py:26
  249.3 10.6 %collective-permute-start.29 = (f32[65536]{0:T(1024)S(1)}, f32[65536]{0:T(1024)S(1)}, u32[]{:S(2)}, u32[]{:S(2)}) collective-permute-start(f32[65536]{0:T(1024)S(1)} %get-tuple-element.253), channel_id=1, source_target_pairs={{0,8},{1,9},{2,10},{3,11},{4,12},{5,13},{6,14},{7,15},{8,16},{9,17... | collective-permute-start | bytes 786440 | tf_op jit(solution)/shard_map/ppermute | solution.py:26
  261.3 17.2 %collective-permute-start.28 = (f32[65536]{0:T(1024)S(1)}, f32[65536]{0:T(1024)S(1)}, u32[]{:S(2)}, u32[]{:S(2)}) collective-permute-start(f32[65536]{0:T(1024)S(1)} %multiply_add_fusion.6), channel_id=1, source_target_pairs={{0,8},{1,9},{2,10},{3,11},{4,12},{5,13},{6,14},{7,15},{8,16},{9,17... | collective-permute-start | bytes 786440 | tf_op jit(solution)/shard_map/ppermute | solution.py:26
  281.8 7.5 %collective-permute-done.31 = f32[65536]{0:T(1024)} collective-permute-done((f32[65536]{0:T(1024)S(1)}, f32[65536]{0:T(1024)}, u32[]{:S(2)}, u32[]{:S(2)}) %collective-permute-start.31) | collective-permute-done | bytes 262176 | tf_op jit(solution)/shard_map/ppermute | solution.py:26
  290.4 6.4 %collective-permute-start.34 = (f32[65536]{0:T(1024)S(1)}, f32[65536]{0:T(1024)S(1)}, u32[]{:S(2)}, u32[]{:S(2)}) collective-permute-start(f32[65536]{0:T(1024)S(1)} %get-tuple-element.252), channel_id=1, source_target_pairs={{0,8},{1,9},{2,10},{3,11},{4,12},{5,13},{6,14},{7,15},{8,16},{9,17... | collective-permute-start | bytes 786440 | tf_op jit(solution)/shard_map/ppermute | solution.py:26
  298.1 7.8 %collective-permute-start.33 = (f32[65536]{0:T(1024)S(1)}, f32[65536]{0:T(1024)S(1)}, u32[]{:S(2)}, u32[]{:S(2)}) collective-permute-start(f32[65536]{0:T(1024)S(1)} %get-tuple-element.250), channel_id=1, source_target_pairs={{0,8},{1,9},{2,10},{3,11},{4,12},{5,13},{6,14},{7,15},{8,16},{9,17... | collective-permute-start | bytes 786440 | tf_op jit(solution)/shard_map/ppermute | solution.py:26
  307.2 8.2 %collective-permute-start.37 = (f32[65536]{0:T(1024)S(1)}, f32[65536]{0:T(1024)S(1)}, u32[]{:S(2)}, u32[]{:S(2)}) collective-permute-start(f32[65536]{0:T(1024)S(1)} %get-tuple-element.248), channel_id=1, source_target_pairs={{0,16},{1,17},{2,18},{3,19},{4,20},{5,21},{6,22},{7,23},{8,24},{9,... | collective-permute-start | bytes 786440 | tf_op jit(solution)/shard_map/ppermute | solution.py:26
  316.7 7.3 %collective-permute-start.36 = (f32[65536]{0:T(1024)S(1)}, f32[65536]{0:T(1024)S(1)}, u32[]{:S(2)}, u32[]{:S(2)}) collective-permute-start(f32[65536]{0:T(1024)S(1)} %multiply_add_fusion.4), channel_id=1, source_target_pairs={{0,16},{1,17},{2,18},{3,19},{4,20},{5,21},{6,22},{7,23},{8,24},{9,... | collective-permute-start | bytes 786440 | tf_op jit(solution)/shard_map/ppermute | solution.py:26
  329.4 10.7 %collective-permute-done.39 = f32[65536]{0:T(1024)} collective-permute-done((f32[65536]{0:T(1024)S(1)}, f32[65536]{0:T(1024)}, u32[]{:S(2)}, u32[]{:S(2)}) %collective-permute-start.39) | collective-permute-done | bytes 262176 | tf_op jit(solution)/shard_map/ppermute | solution.py:26
  346.2 5.5 %collective-permute-start.41 = (f32[65536]{0:T(1024)S(1)}, f32[65536]{0:T(1024)S(1)}, u32[]{:S(2)}, u32[]{:S(2)}) collective-permute-start(f32[65536]{0:T(1024)S(1)} %get-tuple-element.245), channel_id=1, source_target_pairs={{0,16},{1,17},{2,18},{3,19},{4,20},{5,21},{6,22},{7,23},{8,24},{9,... | collective-permute-start | bytes 786440 | tf_op jit(solution)/shard_map/ppermute | solution.py:26
  353.0 7.4 %collective-permute-start.45 = (f32[65536]{0:T(1024)S(1)}, f32[65536]{0:T(1024)S(1)}, u32[]{:S(2)}, u32[]{:S(2)}) collective-permute-start(f32[65536]{0:T(1024)S(1)} %get-tuple-element.243), channel_id=1, source_target_pairs={{0,32},{1,33},{2,34},{3,35},{4,36},{5,37},{6,38},{7,39},{8,40},{9,... | collective-permute-start | bytes 786440 | tf_op jit(solution)/shard_map/ppermute | solution.py:26
  361.8 6.0 %collective-permute-start.44 = (f32[65536]{0:T(1024)S(1)}, f32[65536]{0:T(1024)S(1)}, u32[]{:S(2)}, u32[]{:S(2)}) collective-permute-start(f32[65536]{0:T(1024)S(1)} %multiply_add_fusion.2), channel_id=1, source_target_pairs={{0,32},{1,33},{2,34},{3,35},{4,36},{5,37},{6,38},{7,39},{8,40},{9,... | collective-permute-start | bytes 786440 | tf_op jit(solution)/shard_map/ppermute | solution.py:26
  371.9 6.9 %collective-permute-done.47 = f32[65536]{0:T(1024)S(1)} collective-permute-done((f32[65536]{0:T(1024)S(1)}, f32[65536]{0:T(1024)S(1)}, u32[]{:S(2)}, u32[]{:S(2)}) %collective-permute-start.47) | collective-permute-done | bytes 262176 | tf_op jit(solution)/shard_map/ppermute | solution.py:26
  390.0 7.8 %collective-permute-start.53 = (f32[65536]{0:T(1024)}, f32[65536]{0:T(1024)}, u32[]{:S(2)}, u32[]{:S(2)}) collective-permute-start(f32[65536]{0:T(1024)} %get-tuple-element.238), channel_id=1, source_target_pairs={{0,64},{1,65},{2,66},{3,67},{4,68},{5,69},{6,70},{7,71},{8,72},{9,... | collective-permute-start | bytes 786440 | tf_op jit(solution)/shard_map/ppermute | solution.py:26
  400.2 6.3 %collective-permute-start.52 = (f32[65536]{0:T(1024)}, f32[65536]{0:T(1024)S(1)}, u32[]{:S(2)}, u32[]{:S(2)}) collective-permute-start(f32[65536]{0:T(1024)} %get-tuple-element.351), channel_id=1, source_target_pairs={{0,64},{1,65},{2,66},{3,67},{4,68},{5,69},{6,70},{7,71},{8,72},{9,... | collective-permute-start | bytes 786440 | tf_op jit(solution)/shard_map/ppermute | solution.py:26
  407.8 6.9 %collective-permute-start.57 = (f32[65536]{0:T(1024)}, f32[65536]{0:T(1024)}, u32[]{:S(2)}, u32[]{:S(2)}) collective-permute-start(f32[65536]{0:T(1024)} %get-tuple-element.350), channel_id=1, source_target_pairs={{0,64},{1,65},{2,66},{3,67},{4,68},{5,69},{6,70},{7,71},{8,72},{9,... | collective-permute-start | bytes 786440 | tf_op jit(solution)/shard_map/ppermute | solution.py:26
  417.6 6.0 %collective-permute-done.58 = f32[65536]{0:T(1024)} collective-permute-done((f32[65536]{0:T(1024)}, f32[65536]{0:T(1024)}, u32[]{:S(2)}, u32[]{:S(2)}) %collective-permute-start.58) | collective-permute-done | bytes 262176 | tf_op jit(solution)/shard_map/ppermute | solution.py:26
  425.3 20.0 %collective-permute-start.59 = (f32[65536]{0:T(1024)S(1)}, f32[65536]{0:T(1024)}, u32[]{:S(2)}, u32[]{:S(2)}) collective-permute-start(f32[65536]{0:T(1024)S(1)} %add_divide_fusion), channel_id=1, source_target_pairs={{0,1},{1,2},{2,3},{3,4},{4,5},{5,6},{6,7},{7,8},{8,9},{9,10},{10,1... | collective-permute-start | bytes 786440 | tf_op jit(solution)/shard_map/ppermute | solution.py:26
  445.4 8.3 %slice_reduce_fusion.2 = (f32[3,65536]{1,0:T(4,128)}, f32[3,65536]{1,0:T(4,128)}, f32[3,65536]{1,0:T(4,128)}) fusion(f32[3,3,65536]{2,1,0:T(4,128)S(1)} %copy-done.3), kind=kLoop, calls=%fused_computation.132 | loop fusion | bytes 4718592 | tf_op jit(solution)/shard_map/slice | solution.py:167
  (209 shorter events, 211.1 us)
Async XLA Ops:
  133.9 16.7 %collective-permute-start.5 = (f32[65536]{0:T(1024)S(1)}, f32[65536]{0:T(1024)S(1)}, u32[]{:S(2)}, u32[]{:S(2)}) collective-permute-start(f32[65536]{0:T(1024)S(1)} %add_select_fusion.1), channel_id=1, source_target_pairs={{0,1},{1,2},{2,3},{3,4},{4,5},{5,6},{6,7},{7,8},{8,9},{9,10},{10,1... | collective-permute-start | bytes 786440 | tf_op jit(solution)/shard_map/ppermute | solution.py:26
  150.6 25.3 %collective-permute-start.14 = (f32[65536]{0:T(1024)S(1)}, f32[65536]{0:T(1024)S(1)}, u32[]{:S(2)}, u32[]{:S(2)}) collective-permute-start(f32[65536]{0:T(1024)S(1)} %bitcast.85), channel_id=1, source_target_pairs={{1,0},{2,1},{3,2},{4,3},{5,4},{6,5},{7,6},{8,7},{9,8},{10,9},{11,1... | collective-permute-start | bytes 786440 | tf_op jit(solution)/shard_map/ppermute | solution.py:26
  154.5 22.8 %collective-permute-start.9 = (f32[65536]{0:T(1024)S(1)}, f32[65536]{0:T(1024)S(1)}, u32[]{:S(2)}, u32[]{:S(2)}) collective-permute-start(f32[65536]{0:T(1024)S(1)} %bitcast.82), channel_id=1, source_target_pairs={{0,1},{1,2},{2,3},{3,4},{4,5},{5,6},{6,7},{7,8},{8,9},{9,10},{10,1... | collective-permute-start | bytes 786440 | tf_op jit(solution)/shard_map/ppermute | solution.py:26
  161.2 16.1 %collective-permute-start.12 = (f32[65536]{0:T(1024)S(1)}, f32[65536]{0:T(1024)S(1)}, u32[]{:S(2)}, u32[]{:S(2)}) collective-permute-start(f32[65536]{0:T(1024)S(1)} %multiply_add_fusion.10), channel_id=1, source_target_pairs={{0,2},{1,3},{2,4},{3,5},{4,6},{5,7},{6,8},{7,9},{8,10},{9,11},{10,... | collective-permute-start | bytes 786440 | tf_op jit(solution)/shard_map/ppermute | solution.py:26
  189.8 20.4 %collective-permute-start.18 = (f32[65536]{0:T(1024)S(1)}, f32[65536]{0:T(1024)S(1)}, u32[]{:S(2)}, u32[]{:S(2)}) collective-permute-start(f32[65536]{0:T(1024)S(1)} %get-tuple-element.262), channel_id=1, source_target_pairs={{0,2},{1,3},{2,4},{3,5},{4,6},{5,7},{6,8},{7,9},{8,10},{9,11},{10,... | collective-permute-start | bytes 786440 | tf_op jit(solution)/shard_map/ppermute | solution.py:26
  195.2 16.2 %collective-permute-start.19 = (f32[65536]{0:T(1024)S(1)}, f32[65536]{0:T(1024)S(1)}, u32[]{:S(2)}, u32[]{:S(2)}) collective-permute-start(f32[65536]{0:T(1024)S(1)} %get-tuple-element.260), channel_id=1, source_target_pairs={{2,0},{3,1},{4,2},{5,3},{6,4},{7,5},{8,6},{9,7},{10,8},{11,9},{12,... | collective-permute-start | bytes 786440 | tf_op jit(solution)/shard_map/ppermute | solution.py:26
  196.5 22.4 %collective-permute-start.17 = (f32[65536]{0:T(1024)S(1)}, f32[65536]{0:T(1024)S(1)}, u32[]{:S(2)}, u32[]{:S(2)}) collective-permute-start(f32[65536]{0:T(1024)S(1)} %get-tuple-element.260), channel_id=1, source_target_pairs={{0,2},{1,3},{2,4},{3,5},{4,6},{5,7},{6,8},{7,9},{8,10},{9,11},{10,... | collective-permute-start | bytes 786440 | tf_op jit(solution)/shard_map/ppermute | solution.py:26
  201.3 18.9 %collective-permute-start.22 = (f32[65536]{0:T(1024)S(1)}, f32[65536]{0:T(1024)S(1)}, u32[]{:S(2)}, u32[]{:S(2)}) collective-permute-start(f32[65536]{0:T(1024)S(1)} %get-tuple-element.262), channel_id=1, source_target_pairs={{2,0},{3,1},{4,2},{5,3},{6,4},{7,5},{8,6},{9,7},{10,8},{11,9},{12,... | collective-permute-start | bytes 786440 | tf_op jit(solution)/shard_map/ppermute | solution.py:26
  202.6 17.6 %collective-permute-start.21 = (f32[65536]{0:T(1024)S(1)}, f32[65536]{0:T(1024)S(1)}, u32[]{:S(2)}, u32[]{:S(2)}) collective-permute-start(f32[65536]{0:T(1024)S(1)} %get-tuple-element.258), channel_id=1, source_target_pairs={{0,4},{1,5},{2,6},{3,7},{4,8},{5,9},{6,10},{7,11},{8,12},{9,13},{1... | collective-permute-start | bytes 786440 | tf_op jit(solution)/shard_map/ppermute | solution.py:26
  218.9 16.5 %collective-permute-start.23 = (f32[65536]{0:T(1024)S(1)}, f32[65536]{0:T(1024)}, u32[]{:S(2)}, u32[]{:S(2)}) collective-permute-start(f32[65536]{0:T(1024)S(1)} %multiply_add_fusion.8), channel_id=1, source_target_pairs={{4,0},{5,1},{6,2},{7,3},{8,4},{9,5},{10,6},{11,7},{12,8},{13,9},{1... | collective-permute-start | bytes 786440 | tf_op jit(solution)/shard_map/ppermute | solution.py:26
  236.5 23.4 %collective-permute-start.26 = (f32[65536]{0:T(1024)S(1)}, f32[65536]{0:T(1024)S(1)}, u32[]{:S(2)}, u32[]{:S(2)}) collective-permute-start(f32[65536]{0:T(1024)S(1)} %get-tuple-element.257), channel_id=1, source_target_pairs={{0,4},{1,5},{2,6},{3,7},{4,8},{5,9},{6,10},{7,11},{8,12},{9,13},{1... | collective-permute-start | bytes 786440 | tf_op jit(solution)/shard_map/ppermute | solution.py:26
  238.3 22.9 %collective-permute-start.27 = (f32[65536]{0:T(1024)S(1)}, f32[65536]{0:T(1024)S(1)}, u32[]{:S(2)}, u32[]{:S(2)}) collective-permute-start(f32[65536]{0:T(1024)S(1)} %get-tuple-element.255), channel_id=1, source_target_pairs={{4,0},{5,1},{6,2},{7,3},{8,4},{9,5},{10,6},{11,7},{12,8},{13,9},{1... | collective-permute-start | bytes 786440 | tf_op jit(solution)/shard_map/ppermute | solution.py:26
  239.6 38.9 %collective-permute-start.25 = (f32[65536]{0:T(1024)S(1)}, f32[65536]{0:T(1024)S(1)}, u32[]{:S(2)}, u32[]{:S(2)}) collective-permute-start(f32[65536]{0:T(1024)S(1)} %get-tuple-element.255), channel_id=1, source_target_pairs={{0,4},{1,5},{2,6},{3,7},{4,8},{5,9},{6,10},{7,11},{8,12},{9,13},{1... | collective-permute-start | bytes 786440 | tf_op jit(solution)/shard_map/ppermute | solution.py:26
  248.1 31.8 %collective-permute-start.30 = (f32[65536]{0:T(1024)S(1)}, f32[65536]{0:T(1024)S(1)}, u32[]{:S(2)}, u32[]{:S(2)}) collective-permute-start(f32[65536]{0:T(1024)S(1)} %get-tuple-element.257), channel_id=1, source_target_pairs={{4,0},{5,1},{6,2},{7,3},{8,4},{9,5},{10,6},{11,7},{12,8},{13,9},{1... | collective-permute-start | bytes 786440 | tf_op jit(solution)/shard_map/ppermute | solution.py:26
  249.3 30.5 %collective-permute-start.29 = (f32[65536]{0:T(1024)S(1)}, f32[65536]{0:T(1024)S(1)}, u32[]{:S(2)}, u32[]{:S(2)}) collective-permute-start(f32[65536]{0:T(1024)S(1)} %get-tuple-element.253), channel_id=1, source_target_pairs={{0,8},{1,9},{2,10},{3,11},{4,12},{5,13},{6,14},{7,15},{8,16},{9,17... | collective-permute-start | bytes 786440 | tf_op jit(solution)/shard_map/ppermute | solution.py:26
  259.9 20.3 %collective-permute-start.32 = (f32[65536]{0:T(1024)S(1)}, f32[65536]{0:T(1024)S(1)}, u32[]{:S(2)}, u32[]{:S(2)}) collective-permute-start(f32[65536]{0:T(1024)S(1)} %get-tuple-element.253), channel_id=1, source_target_pairs={{8,0},{9,1},{10,2},{11,3},{12,4},{13,5},{14,6},{15,7},{16,8},{17,9... | collective-permute-start | bytes 786440 | tf_op jit(solution)/shard_map/ppermute | solution.py:26
  261.3 20.5 %collective-permute-start.28 = (f32[65536]{0:T(1024)S(1)}, f32[65536]{0:T(1024)S(1)}, u32[]{:S(2)}, u32[]{:S(2)}) collective-permute-start(f32[65536]{0:T(1024)S(1)} %multiply_add_fusion.6), channel_id=1, source_target_pairs={{0,8},{1,9},{2,10},{3,11},{4,12},{5,13},{6,14},{7,15},{8,16},{9,17... | collective-permute-start | bytes 786440 | tf_op jit(solution)/shard_map/ppermute | solution.py:26
  290.4 25.0 %collective-permute-start.34 = (f32[65536]{0:T(1024)S(1)}, f32[65536]{0:T(1024)S(1)}, u32[]{:S(2)}, u32[]{:S(2)}) collective-permute-start(f32[65536]{0:T(1024)S(1)} %get-tuple-element.252), channel_id=1, source_target_pairs={{0,8},{1,9},{2,10},{3,11},{4,12},{5,13},{6,14},{7,15},{8,16},{9,17... | collective-permute-start | bytes 786440 | tf_op jit(solution)/shard_map/ppermute | solution.py:26
  296.8 19.9 %collective-permute-start.35 = (f32[65536]{0:T(1024)S(1)}, f32[65536]{0:T(1024)S(1)}, u32[]{:S(2)}, u32[]{:S(2)}) collective-permute-start(f32[65536]{0:T(1024)S(1)} %get-tuple-element.250), channel_id=1, source_target_pairs={{8,0},{9,1},{10,2},{11,3},{12,4},{13,5},{14,6},{15,7},{16,8},{17,9... | collective-permute-start | bytes 786440 | tf_op jit(solution)/shard_map/ppermute | solution.py:26
  298.1 26.0 %collective-permute-start.33 = (f32[65536]{0:T(1024)S(1)}, f32[65536]{0:T(1024)S(1)}, u32[]{:S(2)}, u32[]{:S(2)}) collective-permute-start(f32[65536]{0:T(1024)S(1)} %get-tuple-element.250), channel_id=1, source_target_pairs={{0,8},{1,9},{2,10},{3,11},{4,12},{5,13},{6,14},{7,15},{8,16},{9,17... | collective-permute-start | bytes 786440 | tf_op jit(solution)/shard_map/ppermute | solution.py:26
  305.9 19.5 %collective-permute-start.38 = (f32[65536]{0:T(1024)S(1)}, f32[65536]{0:T(1024)S(1)}, u32[]{:S(2)}, u32[]{:S(2)}) collective-permute-start(f32[65536]{0:T(1024)S(1)} %get-tuple-element.252), channel_id=1, source_target_pairs={{8,0},{9,1},{10,2},{11,3},{12,4},{13,5},{14,6},{15,7},{16,8},{17,9... | collective-permute-start | bytes 786440 | tf_op jit(solution)/shard_map/ppermute | solution.py:26
  307.2 18.2 %collective-permute-start.37 = (f32[65536]{0:T(1024)S(1)}, f32[65536]{0:T(1024)S(1)}, u32[]{:S(2)}, u32[]{:S(2)}) collective-permute-start(f32[65536]{0:T(1024)S(1)} %get-tuple-element.248), channel_id=1, source_target_pairs={{0,16},{1,17},{2,18},{3,19},{4,20},{5,21},{6,22},{7,23},{8,24},{9,... | collective-permute-start | bytes 786440 | tf_op jit(solution)/shard_map/ppermute | solution.py:26
  341.2 19.2 %collective-permute-start.42 = (f32[65536]{0:T(1024)S(1)}, f32[65536]{0:T(1024)S(1)}, u32[]{:S(2)}, u32[]{:S(2)}) collective-permute-start(f32[65536]{0:T(1024)S(1)} %get-tuple-element.247), channel_id=1, source_target_pairs={{0,16},{1,17},{2,18},{3,19},{4,20},{5,21},{6,22},{7,23},{8,24},{9,... | collective-permute-start | bytes 786440 | tf_op jit(solution)/shard_map/ppermute | solution.py:26
  344.9 16.8 %collective-permute-start.43 = (f32[65536]{0:T(1024)S(1)}, f32[65536]{0:T(1024)S(1)}, u32[]{:S(2)}, u32[]{:S(2)}) collective-permute-start(f32[65536]{0:T(1024)S(1)} %get-tuple-element.245), channel_id=1, source_target_pairs={{16,0},{17,1},{18,2},{19,3},{20,4},{21,5},{22,6},{23,7},{24,8},{25... | collective-permute-start | bytes 786440 | tf_op jit(solution)/shard_map/ppermute | solution.py:26
  346.2 21.6 %collective-permute-start.41 = (f32[65536]{0:T(1024)S(1)}, f32[65536]{0:T(1024)S(1)}, u32[]{:S(2)}, u32[]{:S(2)}) collective-permute-start(f32[65536]{0:T(1024)S(1)} %get-tuple-element.245), channel_id=1, source_target_pairs={{0,16},{1,17},{2,18},{3,19},{4,20},{5,21},{6,22},{7,23},{8,24},{9,... | collective-permute-start | bytes 786440 | tf_op jit(solution)/shard_map/ppermute | solution.py:26
  351.7 17.5 %collective-permute-start.46 = (f32[65536]{0:T(1024)S(1)}, f32[65536]{0:T(1024)S(1)}, u32[]{:S(2)}, u32[]{:S(2)}) collective-permute-start(f32[65536]{0:T(1024)S(1)} %get-tuple-element.247), channel_id=1, source_target_pairs={{16,0},{17,1},{18,2},{19,3},{20,4},{21,5},{22,6},{23,7},{24,8},{25... | collective-permute-start | bytes 786440 | tf_op jit(solution)/shard_map/ppermute | solution.py:26
  353.0 16.1 %collective-permute-start.45 = (f32[65536]{0:T(1024)S(1)}, f32[65536]{0:T(1024)S(1)}, u32[]{:S(2)}, u32[]{:S(2)}) collective-permute-start(f32[65536]{0:T(1024)S(1)} %get-tuple-element.243), channel_id=1, source_target_pairs={{0,32},{1,33},{2,34},{3,35},{4,36},{5,37},{6,38},{7,39},{8,40},{9,... | collective-permute-start | bytes 786440 | tf_op jit(solution)/shard_map/ppermute | solution.py:26
  379.7 18.2 %collective-permute-start.49 = (f32[65536]{0:T(1024)S(1)}, f32[65536]{0:T(1024)S(1)}, u32[]{:S(2)}, u32[]{:S(2)}) collective-permute-start(f32[65536]{0:T(1024)S(1)} %get-tuple-element.242), channel_id=1, source_target_pairs={{0,32},{1,33},{2,34},{3,35},{4,36},{5,37},{6,38},{7,39},{8,40},{9,... | collective-permute-start | bytes 786440 | tf_op jit(solution)/shard_map/ppermute | solution.py:26
  383.0 16.1 %collective-permute-start.50 = (f32[65536]{0:T(1024)S(1)}, f32[65536]{0:T(1024)S(1)}, u32[]{:S(2)}, u32[]{:S(2)}) collective-permute-start(f32[65536]{0:T(1024)S(1)} %get-tuple-element.240), channel_id=1, source_target_pairs={{0,32},{1,33},{2,34},{3,35},{4,36},{5,37},{6,38},{7,39},{8,40},{9,... | collective-permute-start | bytes 786440 | tf_op jit(solution)/shard_map/ppermute | solution.py:26
  390.0 24.7 %collective-permute-start.53 = (f32[65536]{0:T(1024)}, f32[65536]{0:T(1024)}, u32[]{:S(2)}, u32[]{:S(2)}) collective-permute-start(f32[65536]{0:T(1024)} %get-tuple-element.238), channel_id=1, source_target_pairs={{0,64},{1,65},{2,66},{3,67},{4,68},{5,69},{6,70},{7,71},{8,72},{9,... | collective-permute-start | bytes 786440 | tf_op jit(solution)/shard_map/ppermute | solution.py:26
  397.8 18.1 %collective-permute-start.56 = (f32[65536]{0:T(1024)}, f32[65536]{0:T(1024)}, u32[]{:S(2)}, u32[]{:S(2)}) collective-permute-start(f32[65536]{0:T(1024)} %get-tuple-element.238), channel_id=1, source_target_pairs={{64,0},{65,1},{66,2},{67,3},{68,4},{69,5},{70,6},{71,7},{72,8},{73... | collective-permute-start | bytes 786440 | tf_op jit(solution)/shard_map/ppermute | solution.py:26
  425.3 28.5 %collective-permute-start.59 = (f32[65536]{0:T(1024)S(1)}, f32[65536]{0:T(1024)}, u32[]{:S(2)}, u32[]{:S(2)}) collective-permute-start(f32[65536]{0:T(1024)S(1)} %add_divide_fusion), channel_id=1, source_target_pairs={{0,1},{1,2},{2,3},{3,4},{4,5},{5,6},{6,7},{7,8},{8,9},{9,10},{10,1... | collective-permute-start | bytes 786440 | tf_op jit(solution)/shard_map/ppermute | solution.py:26
  (39 other events, 423.7 us)
where the time goes:
time: 468 us; the launch traced here: 463 us
  starting transfers between devices  244 us (52%)
  waiting for transfers between devices  79.8 us (17%)
  other arithmetic  65 us (14%)
  local copies, waits for them, and re-layouts  60.7 us (13%)
  matrix products  10.9 us (2%)
    ppermute x56, starting transfers between devices, from_behind(): return lax.ppermute(block, axis, route)  232 us
    ppermute x56, waiting for transfers between devices, from_behind(): return lax.ppermute(block, axis, route)  70.2 us
    dynamic_update_slice x6, other arithmetic, thomas(): final, sweeps = lax.scan(forward, (start, start), rows)  21 us
    slice x6, local copies, waits for them, and re-layouts, curvature_of(): along_y = along_y + jnp.roll(extended, 3 - step, 2)  13 us
    select_n x1, other arithmetic, curvature_of(): jnp.where(column_dir == 0, kappa_z, jnp.where(column_dir == 1, kappa_x, j...  11.3 us
  transfers between devices with their start and end apart: 60, of which 21 were waited for; matrix products, arithmetic and copies ran while one was open for 3% of the time, Pallas kernels for 0%

commit v1 on v0

v1 whole, which is shorter than its diff:
```python
import jax
import jax.numpy as jnp
import numpy as np
from jax import lax
from jax.experimental import pallas as pl
from jax.experimental.pallas import tpu as pltpu
from jax.sharding import PartitionSpec as P

TENSION = 0.2
SHIFT_SCALE = 16.0
SIZE = 256
PLANES = 512
SLAB = 4
DEVICES = 128
GROUPS = 16
RING = 4
ROWS = 32
MESH = pl.DeviceIdType.MESH
F32 = jnp.float32
BF16 = jnp.bfloat16


def tables():
    count = np.arange(SIZE)
    angle = 2.0 * np.pi / SIZE * ((count[:, None] * count[None, :]) % SIZE)
    cas = np.cos(angle) + np.sin(angle)
    high = cas.astype(jnp.bfloat16)
    low = (cas - high.astype(np.float64)).astype(jnp.bfloat16)
    waves = (2.0 * np.sin(np.pi * count / SIZE)) ** 2
    excess = waves[:, None] + waves[None, :] + SHIFT_SCALE / float(PLANES * PLANES)
    root = np.sqrt(excess * (excess + 4.0))
    ratio = 2.0 / (2.0 + excess + root)
    weight = -1.0 / (root * SIZE * SIZE)
    return high, low, ratio.astype(np.float32), weight.astype(np.float32)


def split(x):
    high = x.astype(BF16)
    return high, (x - high.astype(F32)).astype(BF16)


def mm(a, b):
    return jnp.dot(a, b, preferred_element_type=F32)


def mm3(ah, al, bh, bl):
    return mm(ah, bh) + (mm(ah, bl) + mm(al, bh))


def up(x, axis):
    return pltpu.roll(x, x.shape[axis] - 1, axis)


def down(x, axis):
    return pltpu.roll(x, 1, axis)


def window7(x, axis):
    size = x.shape[axis]
    three = x + pltpu.roll(x, 1, axis) + pltpu.roll(x, size - 1, axis)
    return x + pltpu.roll(three, 2, axis) + pltpu.roll(three, size - 2, axis)


def bend(da, db, haa, hbb, dab):
    qa = 0.25 * da * da
    qb = 0.25 * db * db
    root = lax.rsqrt(1.0 + qa + qb)
    upper = haa * (1.0 + qb) + hbb * (1.0 + qa) - 0.125 * (da * db * dab)
    return upper * (root * root * root)


def kernel(
    frac_in, dir_in, div_in, th_in, tl_in, ratio_in, weight_in,
    kap_out, pre_out,
    fx, dirs, divs, th, tl, ratio, weight,
    axc, axd, axs, ayc, ayd, ays, kap, shi, slo, spec, pre,
    lus, rc, px, rx, py, ry, od, rd, qx, dx, sd, ab,
    in_sem, out_sem, fs_sem, fr_sem, ks_sem, kr_sem, c_sem, xs_sem, xr_sem, ys_sem, yr_sem,
):
    me = lax.axis_index("gz")
    core = lax.rem(me, 2)
    xpos = lax.rem(lax.div(me, 2), RING)
    group = lax.div(me, 2 * RING)
    sibling = me + 1 - 2 * core
    has_below = me > 0
    has_above = me < DEVICES - 1
    cross = me - 1 + 2 * core
    has_cross = jnp.logical_and(cross >= 0, cross < DEVICES)

    def xpeer(p):
        return group * (2 * RING) + p * 2 + core

    def ypeer(j):
        return j * (2 * RING) + xpos * 2 + core

    loads = [
        pltpu.make_async_copy(frac_in, fx.at[pl.ds(3, SLAB)], in_sem.at[0]),
        pltpu.make_async_copy(dir_in, dirs, in_sem.at[1]),
        pltpu.make_async_copy(div_in, divs, in_sem.at[2]),
        pltpu.make_async_copy(th_in, th, in_sem.at[3]),
        pltpu.make_async_copy(tl_in, tl, in_sem.at[4]),
        pltpu.make_async_copy(ratio_in, ratio, in_sem.at[5]),
        pltpu.make_async_copy(weight_in, weight, in_sem.at[6]),
    ]
    for load in loads:
        load.start()

    barrier = pltpu.get_barrier_semaphore()

    def greet(target):
        pl.semaphore_signal(barrier, inc=1, device_id=(target,), device_id_type=MESH)

    greet(sibling)

    @pl.when(has_cross)
    def _():
        greet(cross)

    for s in range(1, RING):
        greet(xpeer(lax.rem(xpos + s, RING)))

    def greet_group(s, carry):
        greet(ypeer(lax.rem(group + s, GROUPS)))
        return carry

    lax.fori_loop(1, GROUPS, greet_group, 0)
    peers = 1 + (RING - 1) + (GROUPS - 1)
    pl.semaphore_wait(barrier, jnp.where(has_cross, peers + 1, peers))

    def frac_above(j):
        return pltpu.make_async_remote_copy(
            src_ref=frac_in.at[3 - j], dst_ref=fx.at[2 - j], send_sem=fs_sem.at[0, j],
            recv_sem=fr_sem.at[0, j], device_id=(me + 1,), device_id_type=MESH,
        )

    def frac_below(j):
        return pltpu.make_async_remote_copy(
            src_ref=frac_in.at[j], dst_ref=fx.at[7 + j], send_sem=fs_sem.at[1, j],
            recv_sem=fr_sem.at[1, j], device_id=(me - 1,), device_id_type=MESH,
        )

    def kap_above():
        return pltpu.make_async_remote_copy(
            src_ref=kap.at[4], dst_ref=kap.at[0], send_sem=ks_sem.at[0],
            recv_sem=kr_sem.at[0], device_id=(me + 1,), device_id_type=MESH,
        )

    def kap_below():
        return pltpu.make_async_remote_copy(
            src_ref=kap.at[1], dst_ref=kap.at[5], send_sem=ks_sem.at[1],
            recv_sem=kr_sem.at[1], device_id=(me - 1,), device_id_type=MESH,
        )

    @pl.when(has_above)
    def _():
        for j in range(3):
            frac_above(j).start()

    @pl.when(has_below)
    def _():
        for j in range(3):
            frac_below(j).start()

    zero_plane = jnp.zeros((SIZE, SIZE), F32)

    @pl.when(jnp.logical_not(has_below))
    def _():
        for j in range(3):
            fx[j] = zero_plane
        kap[0] = zero_plane

    @pl.when(jnp.logical_not(has_above))
    def _():
        for j in range(3):
            fx[7 + j] = zero_plane
        kap[5] = zero_plane

    def spans(i):
        r0 = pl.multiple_of(i * ROWS, ROWS)
        before = pl.multiple_of(lax.rem(r0 + SIZE - 8, SIZE), 8)
        after = pl.multiple_of(lax.rem(r0 + ROWS, SIZE), 8)
        return r0, before, after

    def wide(ref, t, span):
        r0, before, after = span
        return jnp.concatenate(
            [ref[t, pl.ds(before, 8), :], ref[t, pl.ds(r0, ROWS), :], ref[t, pl.ds(after, 8), :]], axis=0
        )

    def mid(x):
        return x[8 : 8 + ROWS]

    steps = SIZE // ROWS

    def flat_heights(t):
        def body(i, carry):
            span = spans(i)
            rows = pl.ds(span[0], ROWS)
            f = wide(fx, t + 3, span)
            cx = mid(window7(f, 0))
            lift, drop = up(cx, 1), down(cx, 1)
            axc[t + 1, rows, :] = cx
            axd[t + 1, rows, :] = lift - drop
            axs[t + 1, rows, :] = lift + drop - 2.0 * cx
            cy = window7(f, 1)
            lift, drop = mid(up(cy, 0)), mid(down(cy, 0))
            cy = mid(cy)
            ayc[t + 1, rows, :] = cy
            ayd[t + 1, rows, :] = lift - drop
            ays[t + 1, rows, :] = lift + drop - 2.0 * cy
            return carry

        lax.fori_loop(0, steps, body, 0)

    def flat_bend(t):
        def body(i, carry):
            rows = pl.ds(pl.multiple_of(i * ROWS, ROWS), ROWS)
            along_x = dirs[t, rows, :] == 1

            def pick(a, b):
                return jnp.where(along_x, a, b)

            lo = pick(axc[t, rows, :], ayc[t, rows, :])
            at = pick(axc[t + 1, rows, :], ayc[t + 1, rows, :])
            hi = pick(axc[t + 2, rows, :], ayc[t + 2, rows, :])
            d_lo = pick(axd[t, rows, :], ayd[t, rows, :])
            d_at = pick(axd[t + 1, rows, :], ayd[t + 1, rows, :])
            d_hi = pick(axd[t + 2, rows, :], ayd[t + 2, rows, :])
            s_at = pick(axs[t + 1, rows, :], ays[t + 1, rows, :])
            kap[t + 1, rows, :] = bend(hi - lo, d_at, hi + lo - 2.0 * at, s_at, d_hi - d_lo)
            return carry

        lax.fori_loop(0, steps, body, 0)

    def upright_bend(t):
        def body(i, carry):
            span = spans(i)
            rows = pl.ds(span[0], ROWS)
            h = wide(fx, t, span)
            for j in range(1, 7):
                h = h + wide(fx, t + j, span)
            right, left = up(h, 1), down(h, 1)
            db = right - left
            sb = right + left
            center = mid(h)
            plus, minus = mid(up(h, 0)), mid(down(h, 0))
            dab = mid(up(db, 0)) - mid(down(db, 0))
            value = bend(
                plus - minus, mid(db), plus + minus - 2.0 * center, mid(sb) - 2.0 * center, dab
            )
            where = dirs[t, rows, :]
            flat = kap[t + 1, rows, :]
            kap[t + 1, rows, :] = jnp.where(where == 0, value, jnp.where(where == 3, 0.0, flat))
            return carry

        lax.fori_loop(0, steps, body, 0)

    def source(t):
        def body(i, carry):
            span = spans(i)
            rows = pl.ds(span[0], ROWS)
            f = wide(fx, t + 3, span)
            k = wide(kap, t + 1, span)
            face = (k + up(k, 0)) * (up(f, 0) - f)
            total = mid(face) - mid(down(face, 0))
            f, k = mid(f), mid(k)
            face = (k + up(k, 1)) * (up(f, 1) - f)
            total = total + face - down(face, 1)
            total = total + (k + kap[t + 2, rows, :]) * (fx[t + 4, rows, :] - f)
            total = total - (k + kap[t, rows, :]) * (f - fx[t + 2, rows, :])
            value = divs[t, rows, :] + (0.5 * TENSION) * total
            high, low = split(value)
            shi[t, rows, :] = high
            slo[t, rows, :] = low
            return carry

        lax.fori_loop(0, steps, body, 0)

    def transform(t):
        inner = mm3(shi[t], slo[t], th[...], tl[...])
        ih, il = split(inner)
        return mm3(th[...], tl[...], ih, il)

    near = 3 - 3 * core
    step = 2 * core - 1

    def place(d):
        return near + step * d

    near_side = 1 - core
    near_halo = 4 - 5 * core
    far_halo = 5 * core - 1

    def wait_frac(side, j):
        pltpu.make_async_copy(frac_in.at[0], fx.at[0], fr_sem.at[side, j]).wait()

    loads[0].wait()
    lax.fori_loop(0, SLAB, lambda t, c: (flat_heights(t), c)[1], 0)
    loads[1].wait()
    lax.fori_loop(1, 3, lambda t, c: (flat_bend(t), c)[1], 0)
    for j in range(3):
        wait_frac(near_side, j)
    flat_heights(near_halo)
    flat_bend(near)
    upright_bend(near)

    @pl.when(core == 0)
    def _():
        kap_above().start()

    @pl.when(core == 1)
    def _():
        kap_below().start()

    @pl.when(has_cross)
    def _():
        wait_frac(core, 0)

    flat_heights(far_halo)
    flat_bend(place(3))
    upright_bend(place(1))

    @pl.when(has_cross)
    def _():
        wait_frac(core, 1)

    upright_bend(place(2))

    @pl.when(has_cross)
    def _():
        wait_frac(core, 2)

    upright_bend(place(3))

    @pl.when(jnp.logical_and(has_cross, core == 0))
    def _():
        kap_below().start()

    @pl.when(jnp.logical_and(has_cross, core == 1))
    def _():
        kap_above().start()

    out_kap = pltpu.make_async_copy(kap.at[pl.ds(1, SLAB)], kap_out, out_sem.at[0])
    out_kap.start()
    for load in loads[2:]:
        load.wait()

    def forward(d, carry):
        t = place(d)
        source(t)
        spec[t] = transform(t)
        return carry

    def wait_kap(side):
        pltpu.make_async_copy(frac_in.at[0], kap.at[0], kr_sem.at[side]).wait()

    lax.fori_loop(1, 3, forward, 0)
    wait_kap(near_side)
    forward(0, 0)

    @pl.when(has_cross)
    def _():
        wait_kap(core)

    forward(3, 0)

    def sums(half, i):
        rows = pl.ds(pl.multiple_of(half * 128 + i * ROWS, ROWS), ROWS)
        r = ratio[rows, :]
        f = [spec[t, rows, :] for t in range(SLAB)]
        low = r * (f[3] + r * (f[2] + r * (f[1] + r * f[0])))
        high = r * (f[0] + r * (f[1] + r * (f[2] + r * f[3])))
        return low, high

    def sums_out(i, carry):
        rows = pl.ds(pl.multiple_of(i * ROWS, ROWS), ROWS)
        lus[0, rows, :], lus[1, rows, :] = sums(1 - core, i)
        return carry

    lax.fori_loop(0, 4, sums_out, 0)
    send_c = pltpu.make_async_remote_copy(
        src_ref=lus, dst_ref=rc.at[core], send_sem=c_sem.at[0], recv_sem=c_sem.at[1],
        device_id=(sibling,), device_id_type=MESH,
    )
    send_c.start()

    def sums_own(i, carry):
        rows = pl.ds(pl.multiple_of(i * ROWS, ROWS), ROWS)
        rc[core, 0, rows, :], rc[core, 1, rows, :] = sums(core, i)
        return carry

    lax.fori_loop(0, 4, sums_own, 0)
    send_c.wait_recv()

    def power4(x):
        x = x * x
        return x * x

    def pair_rows(p):
        return pl.ds(pl.multiple_of(core * 128 + p * 32, 32), 32), pl.ds(pl.multiple_of(p * 32, 32), 32)

    def combine_pair(p, target, slot):
        table_rows, rows = pair_rows(p)
        rho = power4(ratio[table_rows, :])
        target[slot, 0] = rho * rc[0, 0, rows, :] + rc[1, 0, rows, :]
        target[slot, 1] = rc[0, 1, rows, :] + rho * rc[1, 1, rows, :]

    def send_x(s):
        p = lax.rem(xpos + s, RING)
        return pltpu.make_async_remote_copy(
            src_ref=px.at[p], dst_ref=rx.at[xpos], send_sem=xs_sem.at[0, p],
            recv_sem=xr_sem.at[0, xpos], device_id=(xpeer(p),), device_id_type=MESH,
        )

    for s in (2, 1, 3):
        combine_pair(lax.rem(xpos + s, RING), px, lax.rem(xpos + s, RING))
        send_x(s).start()
    combine_pair(xpos, rx, xpos)

    def wait_x(level, s):
        p = lax.rem(xpos + s, RING)
        pltpu.make_async_copy(px.at[0], rx.at[0], xr_sem.at[level, p]).wait()

    for s in (1, 3, 2):
        wait_x(0, s)

    my_rows = pair_rows(xpos)[0]
    r = ratio[my_rows, :]
    rho2 = power4(r * r)
    low = rx[0, 0]
    high = rx[RING - 1, 1]
    for p in range(1, RING):
        low = rho2 * low + rx[p, 0]
        high = rho2 * high + rx[RING - 1 - p, 1]

    first_half = lax.broadcasted_iota(jnp.int32, (8, 128), 0) < 4

    def swap(x):
        return pltpu.roll(x, 4, 0)

    for i in range(4):
        for lane in range(2):
            lt = low[8 * i : 8 * i + 8, 128 * lane : 128 * lane + 128]
            ut = high[8 * i : 8 * i + 8, 128 * lane : 128 * lane + 128]
            py[i * 4 + lane * 2] = jnp.where(first_half, lt, swap(ut))
            py[i * 4 + lane * 2 + 1] = jnp.where(first_half, swap(lt), ut)

    def send_y(s, level, source_ref, target_ref):
        j = lax.rem(group + s, GROUPS)
        return pltpu.make_async_remote_copy(
            src_ref=source_ref.at[j], dst_ref=target_ref.at[group], send_sem=ys_sem.at[level, j],
            recv_sem=yr_sem.at[level, group], device_id=(ypeer(j),), device_id_type=MESH,
        )

    def exchange_y(level, source_ref, target_ref):
        def go(s, carry):
            send_y(s, level, source_ref, target_ref).start()
            return carry

        lax.fori_loop(1, GROUPS, go, 0)
        target_ref[group] = source_ref[group]

        def wait(s, carry):
            j = lax.rem(group + s, GROUPS)
            pltpu.make_async_copy(py.at[0], ry.at[0], yr_sem.at[level, j]).wait()
            return carry

        lax.fori_loop(1, GROUPS, wait, 0)

    exchange_y(0, py, ry)

    tile_row = lax.div(group, 4)
    tile_lane = lax.rem(lax.div(group, 2), 2)
    tile_half = lax.rem(group, 2)
    rt = ratio[
        pl.ds(pl.multiple_of(core * 128 + xpos * 32 + tile_row * 8, 8), 8),
        pl.ds(pl.multiple_of(tile_lane * 128, 128), 128),
    ]
    keep = first_half == (tile_half == 0)
    rt = jnp.where(keep, rt, swap(rt))
    r32 = power4(power4(rt * rt))
    r513 = power4(power4(r32)) * rt
    merged = [jnp.where(first_half, ry[j], ry[GROUPS - 1 - j]) for j in range(GROUPS)]
    ends = merged[0]
    for j in range(1, GROUPS):
        ends = r32 * ends + merged[j]
    walls = (swap(ends) - r513 * ends) / (1.0 - r513 * r513)
    sweep = [-(rt * walls)]
    for j in range(GROUPS - 1):
        sweep.append(r32 * sweep[j] + merged[j])
    for j in range(GROUPS):
        od[j] = jnp.where(first_half, sweep[j], sweep[GROUPS - 1 - j])

    exchange_y(1, od, rd)

    def gather(index):
        rows = []
        for i in range(4):
            tiles = []
            for lane in range(2):
                t0, t1 = rd[i * 4 + lane * 2], rd[i * 4 + lane * 2 + 1]
                if index == 0:
                    tiles.append(jnp.where(first_half, t0, swap(t1)))
                else:
                    tiles.append(jnp.where(first_half, swap(t0), t1))
            rows.append(jnp.concatenate(tiles, axis=1))
        return jnp.concatenate(rows, axis=0)

    lower = gather(0)
    upper = gather(1)
    for p in range(RING):
        qx[p, 0] = lower
        qx[RING - 1 - p, 1] = upper
        if p < RING - 1:
            lower = rho2 * lower + rx[p, 0]
            upper = rho2 * upper + rx[RING - 1 - p, 1]

    def send_dx(s):
        p = lax.rem(xpos + s, RING)
        return pltpu.make_async_remote_copy(
            src_ref=qx.at[p], dst_ref=dx.at[xpos], send_sem=xs_sem.at[1, p],
            recv_sem=xr_sem.at[1, xpos], device_id=(xpeer(p),), device_id_type=MESH,
        )

    for s in (2, 1, 3):
        send_dx(s).start()
    dx[xpos] = qx[xpos]
    for s in (1, 3, 2):
        wait_x(1, s)

    def spread(p, carry):
        table_rows, rows = pair_rows(p)
        rho = power4(ratio[table_rows, :])
        a, b = dx[p, 0], dx[p, 1]
        a_far = rho * a + rc[0, 0, rows, :]
        b_far = rho * b + rc[1, 1, rows, :]

        @pl.when(core == 0)
        def _():
            ab[0, 0, rows, :] = a
            ab[0, 1, rows, :] = b_far
            sd[0, rows, :] = a_far
            sd[1, rows, :] = b

        @pl.when(core == 1)
        def _():
            ab[1, 0, rows, :] = a_far
            ab[1, 1, rows, :] = b
            sd[0, rows, :] = a
            sd[1, rows, :] = b_far

        return carry

    lax.fori_loop(0, RING, spread, 0)
    send_d = pltpu.make_async_remote_copy(
        src_ref=sd, dst_ref=ab.at[core], send_sem=c_sem.at[2], recv_sem=c_sem.at[3],
        device_id=(sibling,), device_id_type=MESH,
    )
    send_d.start()

    def modal(half):
        def body(i, carry):
            local = pl.ds(pl.multiple_of(i * ROWS, ROWS), ROWS)
            rows = pl.ds(pl.multiple_of(half * 128 + i * ROWS, ROWS), ROWS)
            r = ratio[rows, :]
            w = weight[rows, :]
            f = [spec[t, rows, :] for t in range(SLAB)]
            rising = [ab[half, 0, local, :] + f[0]]
            for t in range(1, SLAB):
                rising.append(r * rising[t - 1] + f[t])
            falling = ab[half, 1, local, :]
            for t in range(SLAB - 1, -1, -1):
                high, low = split(w * (rising[t] + falling))
                shi[t, rows, :] = high
                slo[t, rows, :] = low
                falling = r * (falling + f[t])
            return carry

        lax.fori_loop(0, 4, body, 0)

    modal(core)
    send_d.wait_recv()
    modal(1 - core)

    def out_pre(t):
        return pltpu.make_async_copy(pre.at[t], pre_out.at[t], out_sem.at[1 + t])

    def backward(t, carry):
        pre[t] = transform(t)
        out_pre(t).start()
        return carry

    lax.fori_loop(0, SLAB, backward, 0)

    @pl.when(has_above)
    def _():
        for j in range(3):
            frac_above(j).wait_send()
        kap_above().wait_send()

    @pl.when(has_below)
    def _():
        for j in range(3):
            frac_below(j).wait_send()
        kap_below().wait_send()

    send_c.wait_send()
    send_d.wait_send()
    for s in range(1, RING):
        send_x(s).wait_send()
        send_dx(s).wait_send()

    def drain(s, carry):
        send_y(s, 0, py, ry).wait_send()
        send_y(s, 1, od, rd).wait_send()
        return carry

    lax.fori_loop(1, GROUPS, drain, 0)
    out_kap.wait()
    for t in range(SLAB):
        out_pre(t).wait()


def shards(fraction, column_dir, divergence):
    shape = (SLAB, SIZE, SIZE)
    plane = (SIZE, SIZE)
    high, low, ratio, weight = tables()
    anywhere = pl.BlockSpec(memory_space=pl.ANY)
    vm = pltpu.VMEM
    dma = pltpu.SemaphoreType.DMA
    return pl.pallas_call(
        kernel,
        out_shape=(jax.ShapeDtypeStruct(shape, F32), jax.ShapeDtypeStruct(shape, F32)),
        in_specs=[anywhere] * 7,
        out_specs=(anywhere, anywhere),
        scratch_shapes=[
            vm((10,) + plane, F32), vm(shape, jnp.int32), vm(shape, F32),
            vm(plane, BF16), vm(plane, BF16), vm(plane, F32), vm(plane, F32),
            vm((6,) + plane, F32), vm((6,) + plane, F32), vm((6,) + plane, F32),
            vm((6,) + plane, F32), vm((6,) + plane, F32), vm((6,) + plane, F32),
            vm((6,) + plane, F32), vm(shape, BF16), vm(shape, BF16), vm(shape, F32), vm(shape, F32),
            vm((2, 128, SIZE), F32), vm((2, 2, 128, SIZE), F32),
            vm((4, 2, 32, SIZE), F32), vm((4, 2, 32, SIZE), F32),
            vm((16, 8, 128), F32), vm((16, 8, 128), F32), vm((16, 8, 128), F32), vm((16, 8, 128), F32),
            vm((4, 2, 32, SIZE), F32), vm((4, 2, 32, SIZE), F32),
            vm((2, 128, SIZE), F32), vm((2, 2, 128, SIZE), F32),
            dma((7,)), dma((5,)), dma((2, 3)), dma((2, 3)), dma((2,)), dma((2,)), dma((4,)),
            dma((2, 4)), dma((2, 4)), dma((2, 16)), dma((2, 16)),
        ],
        compiler_params=pltpu.CompilerParams(
            collective_id=0, has_side_effects=True, vmem_limit_bytes=56 * 1024 * 1024
        ),
    )(
        fraction, column_dir, divergence,
        jnp.asarray(high), jnp.asarray(low), jnp.asarray(ratio), jnp.asarray(weight),
    )


def solution(mesh):
    spec = P("gz", None, None)
    return jax.shard_map(
        shards, mesh=mesh, in_specs=(spec, spec, spec), out_specs=(spec, spec), check_vma=False
    )
```

time: 468 us -> 61.9 us (0.13)
  starting transfers between devices: 244 us -> 0 us
  waiting for transfers between devices: 79.8 us -> 0 us
  other arithmetic: 65 us -> 0 us
  Pallas kernels: 0 us -> 57.8 us
  local copies, waits for them, and re-layouts: 60.7 us -> 3.35 us
  matrix products: 10.9 us -> 0 us
    ppermute x60 -> x0, starting transfers between devices: 244 us -> none  [the longest x56 232 us: from_behind(): return lax.ppermute(block, axis, route)]
    ppermute x60 -> x0, waiting for transfers between devices: 79.8 us -> none  [the longest x56 70.2 us: from_behind(): return lax.ppermute(block, axis, route)]
    pallas_call x0 -> x1, Pallas kernels: none -> 57.8 us  [shards(): pl.pallas_call(kernel, out_shape=(jax.ShapeDtypeStruct(shape, F32), jax.S...]
    slice x33 -> x0, local copies, waits for them, and re-layouts: 38.4 us -> none  [the longest x6 13 us: curvature_of(): along_y = along_y + jnp.roll(extended, 3 - step, 2)]
    dynamic_update_slice x6 -> x0, other arithmetic: 21 us -> none  [thomas(): final, sweeps = lax.scan(forward, (start, start), rows)]
    add x15 -> x0, other arithmetic: 18.6 us -> none  [the longest x1 8.2 us: curvature_of(): along_y = along_y + jnp.roll(extended, 3 - step, 2)]
    select_n x5 -> x0, other arithmetic: 14.8 us -> none  [the longest x1 11.3 us: curvature_of(): jnp.where(column_dir == 0, kappa_z, jnp.where(column_dir == 1, kappa_x, j...]
    dot_general x4 -> x0, matrix products: 10.9 us -> none  [the longest x2 5.88 us: hartley_planes(): jnp.einsum('kaj,jb->kab', inner, table_y, precision=lax.Precision.HIGHEST)]
  transfers between devices with their start and end apart: 60 -> 0, of which waited for: 21 -> 0; matrix products, arithmetic and copies ran while one was open for 3% -> 0% of each run, Pallas kernels for 0% -> 0%
where the time goes in v1:
time: 61.9 us; the launch traced here: 61.8 us
  Pallas kernels  57.8 us (93%)
  local copies, waits for them, and re-layouts  3.35 us (5%)
  between operations  0.65 us (1%)
    pallas_call x1, Pallas kernels, shards(): pl.pallas_call(kernel, out_shape=(jax.ShapeDtypeStruct(shape, F32), jax.S...  57.8 us
    unnamed x4, local copies, waits for them, and re-layouts  3.35 us

profile of v1, /device:TPU:1, one launch (start us, length us, event | category | flops | bytes accessed | tf_op | source)
XLA Modules:
  0.0 61.8 jit_solution(6191926894482629088)
XLA Ops:
  0.6 57.8 %shard_map.86 = (f32[4,256,256]{2,1,0:T(8,128)}, f32[4,256,256]{2,1,0:T(8,128)}) custom-call(f32[4,256,256]{2,1,0:T(8,128)} %frac_in.1, s32[4,256,256]{2,1,0:T(8,128)} %dir_in.1, f32[4,256,256]{2,1,0:T(8,128)} %div_in.1, bf16[256,256]{1,0:T(8,128)(2,1)} %constant.8.clone.th_in, bf16[256,256]{1,0:T(8,128)(2,1)} %constant.9.clone.tl_in, ...), custom_call_target="tpu_custom_call" | custom-call | tf_op jit(solution)/shard_map/pallas_call | solution.py:631
  58.4 0.0 copy-start
  58.4 2.4 %copy.11 = f32[4,256,256]{2,1,0:T(8,128)} copy(f32[4,256,256]{2,1,0:T(8,128)} %get-tuple-element.4) | data formatting | bytes 2097152
  60.8 0.0 copy-done
  60.8 1.0 %copy.12 = f32[4,256,256]{2,1,0:T(8,128)} copy(f32[4,256,256]{2,1,0:T(8,128)S(1)} %copy-done) | data formatting | bytes 2097152
Async XLA Ops:
  58.4 2.4 %copy-start = (f32[4,256,256]{2,1,0:T(8,128)S(1)}, f32[4,256,256]{2,1,0:T(8,128)}, u32[]{:S(2)}) copy-start(f32[4,256,256]{2,1,0:T(8,128)} %get-tuple-element.5) | copy-start | bytes 3145732

commit v2 on v1

v2 whole, which is shorter than its diff:
```python
import jax
import jax.numpy as jnp
import numpy as np
from jax import lax
from jax.experimental import pallas as pl
from jax.experimental.pallas import tpu as pltpu
from jax.sharding import PartitionSpec as P

TENSION = 0.2
SHIFT_SCALE = 16.0
SIZE = 256
PLANES = 512
SLAB = 4
DEVICES = 128
CHIPS = 64
ROWS = 32
MESH = pl.DeviceIdType.MESH
F32 = jnp.float32
BF16 = jnp.bfloat16


def tables():
    count = np.arange(SIZE)
    angle = 2.0 * np.pi / SIZE * ((count[:, None] * count[None, :]) % SIZE)
    cas = np.cos(angle) + np.sin(angle)
    high = cas.astype(jnp.bfloat16)
    low = (cas - high.astype(np.float64)).astype(jnp.bfloat16)
    waves = (2.0 * np.sin(np.pi * count / SIZE)) ** 2
    excess = waves[:, None] + waves[None, :] + SHIFT_SCALE / float(PLANES * PLANES)
    root = np.sqrt(excess * (excess + 4.0))
    ratio = 2.0 / (2.0 + excess + root)
    weight = -1.0 / (root * SIZE * SIZE)
    return high, low, ratio.astype(np.float32), weight.astype(np.float32)


def split(x):
    high = x.astype(BF16)
    return high, (x - high.astype(F32)).astype(BF16)


def mm(a, b):
    return jnp.dot(a, b, preferred_element_type=F32)


def mm3(ah, al, bh, bl):
    return mm(ah, bh) + (mm(ah, bl) + mm(al, bh))


def up(x, axis):
    return pltpu.roll(x, x.shape[axis] - 1, axis)


def down(x, axis):
    return pltpu.roll(x, 1, axis)


def window7(x, axis):
    size = x.shape[axis]
    three = x + pltpu.roll(x, 1, axis) + pltpu.roll(x, size - 1, axis)
    return x + pltpu.roll(three, 2, axis) + pltpu.roll(three, size - 2, axis)


def bend(da, db, haa, hbb, dab):
    qa = 0.25 * da * da
    qb = 0.25 * db * db
    root = lax.rsqrt(1.0 + qa + qb)
    upper = haa * (1.0 + qb) + hbb * (1.0 + qa) - 0.125 * (da * db * dab)
    return upper * (root * root * root)


def kernel(
    frac_in, dir_in, div_in, th_in, tl_in, ratio_in, weight_in,
    kap_out, high_out, low_out,
    fx, dirs, divs, th, tl, ratio, weight,
    axc, axd, axs, ayc, ayd, ays, kap, shi, slo, spec, mhi, mlo,
    lus, rc, pu, ru, od, rd, sd, ab,
    in_sem, out_sem, fs_sem, fr_sem, c_sem, u_sem,
):
    me = lax.axis_index("gz")
    core = lax.rem(me, 2)
    chip = lax.div(me, 2)
    sibling = me + 1 - 2 * core
    has_below = me > 0
    has_above = me < DEVICES - 1
    cross = me - 1 + 2 * core
    has_cross = jnp.logical_and(cross >= 0, cross < DEVICES)

    digits = [lax.div(chip, 16), lax.rem(lax.div(chip, 4), 4), lax.rem(chip, 4)]
    parts = [[lax.rem(v + d, 4) * scale for d in range(4)] for v, scale in zip(digits, (16, 4, 1))]
    reach = (0, 1, 2, 1)
    offsets = [(a, b, c) for a in range(4) for b in range(4) for c in range(4) if a or b or c]
    offsets.sort(key=lambda o: -sum(reach[d] for d in o))
    others = [parts[0][a] + parts[1][b] + parts[2][c] for a, b, c in offsets]

    loads = [
        pltpu.make_async_copy(frac_in, fx.at[pl.ds(3, SLAB)], in_sem.at[0]),
        pltpu.make_async_copy(dir_in, dirs, in_sem.at[1]),
        pltpu.make_async_copy(div_in, divs, in_sem.at[2]),
        pltpu.make_async_copy(th_in, th, in_sem.at[3]),
        pltpu.make_async_copy(tl_in, tl, in_sem.at[4]),
        pltpu.make_async_copy(ratio_in, ratio, in_sem.at[5]),
        pltpu.make_async_copy(weight_in, weight, in_sem.at[6]),
    ]
    for load in loads:
        load.start()

    barrier = pltpu.get_barrier_semaphore()

    def greet(target):
        pl.semaphore_signal(barrier, inc=1, device_id=(target,), device_id_type=MESH)

    greet(sibling)

    @pl.when(has_cross)
    def _():
        greet(cross)

    for other in others:
        greet(2 * other + core)

    peers = 1 + (CHIPS - 1)
    pl.semaphore_wait(barrier, jnp.where(has_cross, peers + 1, peers))

    def frac_above(j):
        return pltpu.make_async_remote_copy(
            src_ref=frac_in.at[3 - j], dst_ref=fx.at[2 - j], send_sem=fs_sem.at[0, j],
            recv_sem=fr_sem.at[0, j], device_id=(me + 1,), device_id_type=MESH,
        )

    def frac_below(j):
        return pltpu.make_async_remote_copy(
            src_ref=frac_in.at[j], dst_ref=fx.at[7 + j], send_sem=fs_sem.at[1, j],
            recv_sem=fr_sem.at[1, j], device_id=(me - 1,), device_id_type=MESH,
        )

    @pl.when(has_above)
    def _():
        for j in range(3):
            frac_above(j).start()

    @pl.when(has_below)
    def _():
        for j in range(3):
            frac_below(j).start()

    zero_plane = jnp.zeros((SIZE, SIZE), F32)

    @pl.when(jnp.logical_not(has_below))
    def _():
        for j in range(3):
            fx[j] = zero_plane

    @pl.when(jnp.logical_not(has_above))
    def _():
        for j in range(3):
            fx[7 + j] = zero_plane

    def flat_heights(t):
        f = fx[t + 3]
        cx = window7(f, 0)
        lift, drop = up(cx, 1), down(cx, 1)
        axc[t + 1] = cx
        axd[t + 1] = lift - drop
        axs[t + 1] = lift + drop - 2.0 * cx
        cy = window7(f, 1)
        lift, drop = up(cy, 0), down(cy, 0)
        ayc[t + 1] = cy
        ayd[t + 1] = lift - drop
        ays[t + 1] = lift + drop - 2.0 * cy

    def flat_bend(t):
        along_x = dirs[t] == 1

        def pick(a, b):
            return jnp.where(along_x, a, b)

        lo = pick(axc[t], ayc[t])
        at = pick(axc[t + 1], ayc[t + 1])
        hi = pick(axc[t + 2], ayc[t + 2])
        d_lo = pick(axd[t], ayd[t])
        d_at = pick(axd[t + 1], ayd[t + 1])
        d_hi = pick(axd[t + 2], ayd[t + 2])
        s_at = pick(axs[t + 1], ays[t + 1])
        kap[t] = bend(hi - lo, d_at, hi + lo - 2.0 * at, s_at, d_hi - d_lo)

    def upright_bend(t):
        h = fx[t]
        for j in range(1, 7):
            h = h + fx[t + j]
        right, left = up(h, 1), down(h, 1)
        db = right - left
        sb = right + left
        plus, minus = up(h, 0), down(h, 0)
        dab = up(db, 0) - down(db, 0)
        value = bend(plus - minus, db, plus + minus - 2.0 * h, sb - 2.0 * h, dab)
        where = dirs[t]
        kap[t] = jnp.where(where == 0, value, jnp.where(where == 3, 0.0, kap[t]))

    def store(t, value):
        shi[t + 1], slo[t + 1] = split(value)

    def source(t):
        f = fx[t + 3]
        k = kap[t]
        face = (k + up(k, 0)) * (up(f, 0) - f)
        total = face - down(face, 0)
        face = (k + up(k, 1)) * (up(f, 1) - f)
        total = total + face - down(face, 1)
        above = jnp.where(t == SLAB - 1, 0.0, kap[jnp.minimum(t + 1, SLAB - 1)])
        below = jnp.where(t == 0, 0.0, kap[jnp.maximum(t - 1, 0)])
        total = total + (k + above) * (fx[t + 4] - f) - (k + below) * (f - fx[t + 2])
        store(t, divs[t] + (0.5 * TENSION) * total)

    def beyond(t, outer, exists):
        scale = jnp.where(exists, 0.5 * TENSION, 0.0)
        store(outer, scale * kap[t] * (fx[t + 3] - fx[outer + 3]))

    def transform(t):
        inner = mm3(shi[t + 1], slo[t + 1], th[...], tl[...])
        ih, il = split(inner)
        spec[t + 1] = mm3(th[...], tl[...], ih, il)

    near = 3 - 3 * core
    step = 2 * core - 1

    def place(d):
        return near + step * d

    near_side = 1 - core
    near_halo = 4 - 5 * core
    far_halo = 5 * core - 1

    def wait_frac(side, j):
        pltpu.make_async_copy(frac_in.at[0], fx.at[0], fr_sem.at[side, j]).wait()

    def wait_far(j):
        @pl.when(has_cross)
        def _():
            wait_frac(core, j)

    loads[0].wait()
    lax.fori_loop(0, SLAB, lambda t, c: (flat_heights(t), c)[1], 0)
    loads[1].wait()
    lax.fori_loop(1, 3, lambda t, c: (flat_bend(t), c)[1], 0)
    for j in range(3):
        wait_frac(near_side, j)
    flat_heights(near_halo)
    flat_bend(near)
    upright_bend(near)
    for load in loads[2:]:
        load.wait()
    beyond(near, near_halo, True)
    transform(near_halo)
    wait_far(0)
    flat_heights(far_halo)
    flat_bend(place(3))
    upright_bend(place(1))
    source(near)
    transform(near)
    wait_far(1)
    upright_bend(place(2))
    source(place(1))
    transform(place(1))
    wait_far(2)
    upright_bend(place(3))
    out_kap = pltpu.make_async_copy(kap, kap_out, out_sem.at[0])
    out_kap.start()
    beyond(place(3), far_halo, has_cross)
    source(place(2))
    source(place(3))
    transform(place(2))
    transform(place(3))
    transform(far_halo)

    def sums(half, i):
        rows = pl.ds(pl.multiple_of(half * 128 + i * ROWS, ROWS), ROWS)
        r = ratio[rows, :]
        f = [spec[t, rows, :] for t in range(SLAB + 2)]
        low, high = f[0], f[SLAB + 1]
        for t in range(1, SLAB + 1):
            low = r * low + f[t]
            high = r * high + f[SLAB + 1 - t]
        low = r * low + f[SLAB + 1]
        high = r * high + f[0]
        return low, high

    def sums_out(i, carry):
        rows = pl.ds(pl.multiple_of(i * ROWS, ROWS), ROWS)
        lus[0, rows, :], lus[1, rows, :] = sums(1 - core, i)
        return carry

    lax.fori_loop(0, 4, sums_out, 0)
    send_c = pltpu.make_async_remote_copy(
        src_ref=lus, dst_ref=rc.at[core], send_sem=c_sem.at[0], recv_sem=c_sem.at[1],
        device_id=(sibling,), device_id_type=MESH,
    )
    send_c.start()

    def sums_own(i, carry):
        rows = pl.ds(pl.multiple_of(i * ROWS, ROWS), ROWS)
        rc[core, 0, rows, :], rc[core, 1, rows, :] = sums(core, i)
        return carry

    lax.fori_loop(0, 4, sums_own, 0)
    send_c.wait_recv()

    def power4(x):
        x = x * x
        return x * x

    first_half = lax.broadcasted_iota(jnp.int32, (8, 128), 0) < 4

    def swap(x):
        return pltpu.roll(x, 4, 0)

    def cut(i, carry):
        rows = pl.ds(pl.multiple_of(i * 8, 8), 8)
        rho = power4(ratio[pl.ds(pl.multiple_of(core * 128 + i * 8, 8), 8), :])
        low = rho * rc[0, 0, rows, :] + rc[1, 0, rows, :]
        high = rc[0, 1, rows, :] + rho * rc[1, 1, rows, :]
        for lane in range(2):
            lt = low[:, 128 * lane : 128 * lane + 128]
            ut = high[:, 128 * lane : 128 * lane + 128]
            pu[i * 4 + lane * 2] = jnp.where(first_half, lt, swap(ut))
            pu[i * 4 + lane * 2 + 1] = jnp.where(first_half, swap(lt), ut)
        return carry

    lax.fori_loop(0, 16, cut, 0, unroll=4)

    def send_part(other, level, source_ref, target_ref):
        return pltpu.make_async_remote_copy(
            src_ref=source_ref.at[other], dst_ref=target_ref.at[chip], send_sem=u_sem.at[level, 0],
            recv_sem=u_sem.at[level, 1], device_id=(2 * other + core,), device_id_type=MESH,
        )

    def wait_parts(level, way):
        span = pl.ds(0, CHIPS - 1)
        pltpu.make_async_copy(pu.at[span], ru.at[span], u_sem.at[level, way]).wait()

    for other in others:
        send_part(other, 0, pu, ru).start()
    ru[chip] = pu[chip]
    wait_parts(0, 1)

    tile_row = lax.div(chip, 4)
    tile_lane = lax.rem(lax.div(chip, 2), 2)
    tile_half = lax.rem(chip, 2)
    rt = ratio[
        pl.ds(pl.multiple_of(core * 128 + tile_row * 8, 8), 8),
        pl.ds(pl.multiple_of(tile_lane * 128, 128), 128),
    ]
    keep = first_half == (tile_half == 0)
    rt = jnp.where(keep, rt, swap(rt))
    r8 = power4(rt * rt)
    r64 = power4(r8 * r8)
    r513 = power4(r64 * r64) * rt
    merged = [jnp.where(first_half, ru[j], ru[CHIPS - 1 - j]) for j in range(CHIPS)]
    blocks = []
    for b in range(8):
        total = merged[8 * b]
        for j in range(1, 8):
            total = r8 * total + merged[8 * b + j]
        blocks.append(total)
    ends = blocks[0]
    for b in range(1, 8):
        ends = r64 * ends + blocks[b]
    walls = (swap(ends) - r513 * ends) / (1.0 - r513 * r513)
    starts = [-(rt * walls)]
    for b in range(7):
        starts.append(r64 * starts[b] + blocks[b])
    sweep = []
    for b in range(8):
        sweep.append(starts[b])
        for j in range(7):
            sweep.append(r8 * sweep[-1] + merged[8 * b + j])
    for j in range(CHIPS):
        od[j] = jnp.where(first_half, sweep[j], sweep[CHIPS - 1 - j])

    for other in others:
        send_part(other, 1, od, rd).start()
    rd[chip] = od[chip]
    wait_parts(1, 1)

    def spread(i, carry):
        rows = pl.ds(pl.multiple_of(i * 8, 8), 8)
        rho = power4(ratio[pl.ds(pl.multiple_of(core * 128 + i * 8, 8), 8), :])
        tiles = [rd[i * 4 + k] for k in range(4)]
        a = jnp.concatenate([jnp.where(first_half, tiles[k], swap(tiles[k + 1])) for k in (0, 2)], axis=1)
        b = jnp.concatenate([jnp.where(first_half, swap(tiles[k]), tiles[k + 1]) for k in (0, 2)], axis=1)
        a_far = rho * a + rc[0, 0, rows, :]
        b_far = rho * b + rc[1, 1, rows, :]
        even = core == 0
        ab[core, 0, rows, :] = jnp.where(even, a, a_far)
        ab[core, 1, rows, :] = jnp.where(even, b_far, b)
        sd[0, rows, :] = jnp.where(even, a_far, a)
        sd[1, rows, :] = jnp.where(even, b, b_far)
        return carry

    lax.fori_loop(0, 16, spread, 0, unroll=4)
    send_d = pltpu.make_async_remote_copy(
        src_ref=sd, dst_ref=ab.at[core], send_sem=c_sem.at[2], recv_sem=c_sem.at[3],
        device_id=(sibling,), device_id_type=MESH,
    )
    send_d.start()

    def modal(half):
        def body(i, carry):
            local = pl.ds(pl.multiple_of(i * ROWS, ROWS), ROWS)
            rows = pl.ds(pl.multiple_of(half * 128 + i * ROWS, ROWS), ROWS)
            r = ratio[rows, :]
            w = weight[rows, :]
            f = [spec[t, rows, :] for t in range(SLAB + 2)]
            rising = [r * f[0] + ab[half, 0, local, :] + f[1]]
            for t in range(1, SLAB):
                rising.append(r * rising[t - 1] + f[t + 1])
            falling = ab[half, 1, local, :] + r * f[SLAB + 1]
            for t in range(SLAB - 1, -1, -1):
                mhi[t, rows, :], mlo[t, rows, :] = split(w * (rising[t] + falling))
                falling = r * (falling + f[t + 1])
            return carry

        lax.fori_loop(0, 4, body, 0, unroll=2)

    modal(core)
    send_d.wait_recv()
    modal(1 - core)

    out_high = pltpu.make_async_copy(mhi, high_out, out_sem.at[1])
    out_low = pltpu.make_async_copy(mlo, low_out, out_sem.at[2])
    out_high.start()
    out_low.start()

    @pl.when(has_above)
    def _():
        for j in range(3):
            frac_above(j).wait_send()

    @pl.when(has_below)
    def _():
        for j in range(3):
            frac_below(j).wait_send()

    send_c.wait_send()
    send_d.wait_send()
    wait_parts(0, 0)
    wait_parts(1, 0)
    out_kap.wait()
    out_high.wait()
    out_low.wait()


def finish(kap_in, high_in, low_in, th_in, tl_in, kap_out, pre_out, mhi, mlo, th, tl, pre, sem):
    passing = pltpu.make_async_copy(kap_in, kap_out, sem.at[0])
    passing.start()
    loads = [
        pltpu.make_async_copy(source, target, sem.at[1 + i])
        for i, (source, target) in enumerate(((th_in, th), (tl_in, tl), (high_in, mhi), (low_in, mlo)))
    ]
    for load in loads:
        load.start()
    for load in loads:
        load.wait()
    stores = []
    for t in range(SLAB):
        ih, il = split(mm3(mhi[t], mlo[t], th[...], tl[...]))
        pre[t] = mm3(th[...], tl[...], ih, il)
        stores.append(pltpu.make_async_copy(pre.at[t], pre_out.at[t], sem.at[5 + t]))
        stores[t].start()
    passing.wait()
    for copy in stores:
        copy.wait()


def shards(fraction, column_dir, divergence):
    shape = (SLAB, SIZE, SIZE)
    plane = (SIZE, SIZE)
    high, low, ratio, weight = tables()
    anywhere = pl.BlockSpec(memory_space=pl.ANY)
    vm = pltpu.VMEM
    dma = pltpu.SemaphoreType.DMA
    high, low = jnp.asarray(high), jnp.asarray(low)
    whole = jax.ShapeDtypeStruct(shape, F32)
    half = jax.ShapeDtypeStruct(shape, BF16)
    params = dict(vmem_limit_bytes=56 * 1024 * 1024)
    six = vm((SLAB + 2,) + plane, F32)
    curvature, modal_high, modal_low = pl.pallas_call(
        kernel,
        out_shape=(whole, half, half),
        in_specs=[anywhere] * 7,
        out_specs=(anywhere,) * 3,
        scratch_shapes=[
            vm((10,) + plane, F32), vm(shape, jnp.int32), vm(shape, F32),
            vm(plane, BF16), vm(plane, BF16), vm(plane, F32), vm(plane, F32),
            six, six, six, six, six, six,
            vm(shape, F32), vm((SLAB + 2,) + plane, BF16), vm((SLAB + 2,) + plane, BF16), six,
            vm(shape, BF16), vm(shape, BF16),
            vm((2, 128, SIZE), F32), vm((2, 2, 128, SIZE), F32),
            vm((CHIPS, 8, 128), F32), vm((CHIPS, 8, 128), F32),
            vm((CHIPS, 8, 128), F32), vm((CHIPS, 8, 128), F32),
            vm((2, 128, SIZE), F32), vm((2, 2, 128, SIZE), F32),
            dma((7,)), dma((3,)), dma((2, 3)), dma((2, 3)), dma((4,)), dma((2, 2)),
        ],
        compiler_params=pltpu.CompilerParams(collective_id=0, has_side_effects=True, **params),
    )(fraction, column_dir, divergence, high, low, jnp.asarray(ratio), jnp.asarray(weight))
    return pl.pallas_call(
        finish,
        out_shape=(whole, whole),
        in_specs=[anywhere] * 5,
        out_specs=(anywhere,) * 2,
        scratch_shapes=[
            vm(shape, BF16), vm(shape, BF16), vm(plane, BF16), vm(plane, BF16), vm(shape, F32), dma((9,)),
        ],
        compiler_params=pltpu.CompilerParams(**params),
    )(curvature, modal_high, modal_low, high, low)


def solution(mesh):
    spec = P("gz", None, None)
    return jax.shard_map(
        shards, mesh=mesh, in_specs=(spec, spec, spec), out_specs=(spec, spec), check_vma=False
    )
```

time: 61.9 us -> 75.3 us (1.22)
  Pallas kernels: 57.8 us -> 74.5 us
  local copies, waits for them, and re-layouts: 3.35 us -> 0 us
    pallas_call x1 -> x2, Pallas kernels: 57.8 us -> 74.5 us  [the longest x1 41.5 us: shards(): pl.pallas_call(kernel, out_shape=(whole, half, half), in_specs=[anywhere]...]
    unnamed x4 -> x0, local copies, waits for them, and re-layouts: 3.35 us -> none
where the time goes in v2:
time: 75.3 us; the launch traced here: 75.1 us
  Pallas kernels  74.5 us (99%)
    pallas_call x1, Pallas kernels, shards(): pl.pallas_call(kernel, out_shape=(whole, half, half), in_specs=[anywhere]...  41.5 us
    pallas_call x1, Pallas kernels, shards(): pl.pallas_call(finish, out_shape=(whole, whole), in_specs=[anywhere] * 5,...  33 us

profile of v2, /device:TPU:1, one launch (start us, length us, event | category | flops | bytes accessed | tf_op | source)
XLA Modules:
  0.0 75.1 jit_solution(16116723711986547326)
XLA Ops:
  0.6 41.5 %shard_map.86 = (f32[4,256,256]{2,1,0:T(8,128)}, bf16[4,256,256]{2,1,0:T(8,128)(2,1)}, bf16[4,256,256]{2,1,0:T(8,128)(2,1)}) custom-call(f32[4,256,256]{2,1,0:T(8,128)} %frac_in.1, s32[4,256,256]{2,1,0:T(8,128)} %dir_in.1, f32[4,256,256]{2,1,0:T(8,128)} %div_in.1, bf16[256,256]{1,0:T(8,128)(2,1)} %constant.8.clone.th_in, ...), custom_call_target="tpu_custom_call" | custom-call | tf_op jit(solution)/shard_map/pallas_call | solution.py:486
  42.2 33.0 %shard_map.87 = (f32[4,256,256]{2,1,0:T(8,128)}, f32[4,256,256]{2,1,0:T(8,128)}) custom-call(f32[4,256,256]{2,1,0:T(8,128)} %get-tuple-element.5.kap_in, bf16[4,256,256]{2,1,0:T(8,128)(2,1)} %get-tuple-element.6.high_in, bf16[4,256,256]{2,1,0:T(8,128)(2,1)} %get-tuple-element.7.low_in, bf16[256,256]{1,0:T(8,128)(2,1)} %constant.8.clone.th_in, ...), custom_call_target="tpu_custom_call" | custom-call | tf_op jit(solution)/shard_map/pallas_call | solution.py:505

commit v3 on v2

--- a/solution.py
+++ b/solution.py
@@ -449,17 +449,20 @@
     out_low.wait()
 
 
-def finish(kap_in, high_in, low_in, th_in, tl_in, kap_out, pre_out, mhi, mlo, th, tl, pre, sem):
-    passing = pltpu.make_async_copy(kap_in, kap_out, sem.at[0])
-    passing.start()
+def finish(kap_in, high_in, low_in, th_in, tl_in, kap_out, pre_out, kap, mhi, mlo, th, tl, pre, sem):
     loads = [
         pltpu.make_async_copy(source, target, sem.at[1 + i])
         for i, (source, target) in enumerate(((th_in, th), (tl_in, tl), (high_in, mhi), (low_in, mlo)))
     ]
+    fetch = pltpu.make_async_copy(kap_in, kap, sem.at[0])
+    passing = pltpu.make_async_copy(kap, kap_out, sem.at[9])
     for load in loads:
         load.start()
+    fetch.start()
     for load in loads:
         load.wait()
+    fetch.wait()
+    passing.start()
     stores = []
     for t in range(SLAB):
         ih, il = split(mm3(mhi[t], mlo[t], th[...], tl[...]))
@@ -508,7 +511,7 @@
         in_specs=[anywhere] * 5,
         out_specs=(anywhere,) * 2,
         scratch_shapes=[
-            vm(shape, BF16), vm(shape, BF16), vm(plane, BF16), vm(plane, BF16), vm(shape, F32), dma((9,)),
+            vm(shape, F32), vm(shape, BF16), vm(shape, BF16), vm(plane, BF16), vm(plane, BF16), vm(shape, F32), dma((10,)),
         ],
         compiler_params=pltpu.CompilerParams(**params),
     )(curvature, modal_high, modal_low, high, low)

time: 75.3 us -> 46.1 us (0.61)
  Pallas kernels: 74.5 us -> 45.3 us
    pallas_call x1, Pallas kernels: 33 us -> 3.76 us  [shards(): pl.pallas_call(finish, out_shape=(whole, whole), in_specs=[anywhere] * 5,...]
where the time goes in v3:
time: 46.1 us; the launch traced here: 45.9 us
  Pallas kernels  45.3 us (98%)
  between operations  0.64 us (1%)
    pallas_call x1, Pallas kernels, shards(): pl.pallas_call(kernel, out_shape=(whole, half, half), in_specs=[anywhere]...  41.5 us
    pallas_call x1, Pallas kernels, shards(): pl.pallas_call(finish, out_shape=(whole, whole), in_specs=[anywhere] * 5,...  3.76 us

profile of v3, /device:TPU:1, one launch (start us, length us, event | category | flops | bytes accessed | tf_op | source)
XLA Modules:
  0.0 45.9 jit_solution(6834116308326743839)
XLA Ops:
  0.6 41.5 %shard_map.86 = (f32[4,256,256]{2,1,0:T(8,128)}, bf16[4,256,256]{2,1,0:T(8,128)(2,1)}, bf16[4,256,256]{2,1,0:T(8,128)(2,1)}) custom-call(f32[4,256,256]{2,1,0:T(8,128)} %frac_in.1, s32[4,256,256]{2,1,0:T(8,128)} %dir_in.1, f32[4,256,256]{2,1,0:T(8,128)} %div_in.1, bf16[256,256]{1,0:T(8,128)(2,1)} %constant.8.clone.th_in, ...), custom_call_target="tpu_custom_call" | custom-call | tf_op jit(solution)/shard_map/pallas_call | solution.py:489
  42.2 3.8 %shard_map.87 = (f32[4,256,256]{2,1,0:T(8,128)}, f32[4,256,256]{2,1,0:T(8,128)}) custom-call(f32[4,256,256]{2,1,0:T(8,128)} %get-tuple-element.5.kap_in, bf16[4,256,256]{2,1,0:T(8,128)(2,1)} %get-tuple-element.6.high_in, bf16[4,256,256]{2,1,0:T(8,128)(2,1)} %get-tuple-element.7.low_in, bf16[256,256]{1,0:T(8,128)(2,1)} %constant.8.clone.th_in, ...), custom_call_target="tpu_custom_call" | custom-call | tf_op jit(solution)/shard_map/pallas_call | solution.py:508

commit v4 on v3

--- a/solution.py
+++ b/solution.py
@@ -74,7 +74,7 @@
     fx, dirs, divs, th, tl, ratio, weight,
     axc, axd, axs, ayc, ayd, ays, kap, shi, slo, spec, mhi, mlo,
     lus, rc, pu, ru, od, rd, sd, ab,
-    in_sem, out_sem, fs_sem, fr_sem, c_sem, u_sem,
+    in_sem, out_sem, fs_sem, fr_sem, c_sem, u_sem, round_sem,
 ):
     me = lax.axis_index("gz")
     core = lax.rem(me, 2)
@@ -90,7 +90,14 @@
     reach = (0, 1, 2, 1)
     offsets = [(a, b, c) for a in range(4) for b in range(4) for c in range(4) if a or b or c]
     offsets.sort(key=lambda o: -sum(reach[d] for d in o))
-    others = [parts[0][a] + parts[1][b] + parts[2][c] for a, b, c in offsets]
+
+    def chips_at(places):
+        return [parts[0][a] + parts[1][b] + parts[2][c] for a, b, c in places]
+
+    others = chips_at(offsets)
+    nearest = chips_at([(1, 0, 0), (3, 0, 0), (0, 1, 0), (0, 3, 0), (0, 0, 1), (0, 0, 3)])
+    y_ring = chips_at([(0, 2, 0), (0, 1, 0), (0, 3, 0)])
+    z_ring = chips_at([(2, 0, 0), (1, 0, 0), (3, 0, 0)])
 
     loads = [
         pltpu.make_async_copy(frac_in, fx.at[pl.ds(3, SLAB)], in_sem.at[0]),
@@ -115,11 +122,17 @@
     def _():
         greet(cross)
 
-    for other in others:
+    for other in nearest:
         greet(2 * other + core)
 
-    peers = 1 + (CHIPS - 1)
+    peers = 1 + len(nearest)
     pl.semaphore_wait(barrier, jnp.where(has_cross, peers + 1, peers))
+
+    def hail(i, chips):
+        for other in chips:
+            pl.semaphore_signal(
+                round_sem.at[i], inc=1, device_id=(2 * other + core,), device_id_type=MESH
+            )
 
     def frac_above(j):
         return pltpu.make_async_remote_copy(
@@ -143,6 +156,7 @@
         for j in range(3):
             frac_below(j).start()
 
+    hail(0, nearest)
     zero_plane = jnp.zeros((SIZE, SIZE), F32)
 
     @pl.when(jnp.logical_not(has_below))
@@ -240,6 +254,8 @@
 
     loads[0].wait()
     lax.fori_loop(0, SLAB, lambda t, c: (flat_heights(t), c)[1], 0)
+    pl.semaphore_wait(round_sem.at[0], len(nearest))
+    hail(1, y_ring)
     loads[1].wait()
     lax.fori_loop(1, 3, lambda t, c: (flat_bend(t), c)[1], 0)
     for j in range(3):
@@ -251,6 +267,8 @@
         load.wait()
     beyond(near, near_halo, True)
     transform(near_halo)
+    pl.semaphore_wait(round_sem.at[1], len(y_ring))
+    hail(2, z_ring)
     wait_far(0)
     flat_heights(far_halo)
     flat_bend(place(3))
@@ -337,6 +355,7 @@
         span = pl.ds(0, CHIPS - 1)
         pltpu.make_async_copy(pu.at[span], ru.at[span], u_sem.at[level, way]).wait()
 
+    pl.semaphore_wait(round_sem.at[2], len(z_ring))
     for other in others:
         send_part(other, 0, pu, ru).start()
     ru[chip] = pu[chip]
@@ -501,7 +520,7 @@
             vm((CHIPS, 8, 128), F32), vm((CHIPS, 8, 128), F32),
             vm((CHIPS, 8, 128), F32), vm((CHIPS, 8, 128), F32),
             vm((2, 128, SIZE), F32), vm((2, 2, 128, SIZE), F32),
-            dma((7,)), dma((3,)), dma((2, 3)), dma((2, 3)), dma((4,)), dma((2, 2)),
+            dma((7,)), dma((3,)), dma((2, 3)), dma((2, 3)), dma((4,)), dma((2, 2)), pltpu.SemaphoreType.REGULAR((3,)),
         ],
         compiler_params=pltpu.CompilerParams(collective_id=0, has_side_effects=True, **params),
     )(fraction, column_dir, divergence, high, low, jnp.asarray(ratio), jnp.asarray(weight))

time: 46.1 us -> 43.5 us (0.944)
  Pallas kernels: 45.3 us -> 42.8 us
    pallas_call x1, Pallas kernels: 41.5 us -> 39 us  [shards(): pl.pallas_call(kernel, out_shape=(whole, half, half), in_specs=[anywhere]...]
where the time goes in v4:
time: 43.5 us; the launch traced here: 43.4 us
  Pallas kernels  42.8 us (98%)
  between operations  0.64 us (1%)
    pallas_call x1, Pallas kernels, shards(): pl.pallas_call(kernel, out_shape=(whole, half, half), in_specs=[anywhere]...  39 us
    pallas_call x1, Pallas kernels, shards(): pl.pallas_call(finish, out_shape=(whole, whole), in_specs=[anywhere] * 5,...  3.76 us

profile of v4, /device:TPU:1, one launch (start us, length us, event | category | flops | bytes accessed | tf_op | source)
XLA Modules:
  0.0 43.4 jit_solution(13274797297224967632)
XLA Ops:
  0.6 39.0 %shard_map.86 = (f32[4,256,256]{2,1,0:T(8,128)}, bf16[4,256,256]{2,1,0:T(8,128)(2,1)}, bf16[4,256,256]{2,1,0:T(8,128)(2,1)}) custom-call(f32[4,256,256]{2,1,0:T(8,128)} %frac_in.1, s32[4,256,256]{2,1,0:T(8,128)} %dir_in.1, f32[4,256,256]{2,1,0:T(8,128)} %div_in.1, bf16[256,256]{1,0:T(8,128)(2,1)} %constant.8.clone.th_in, ...), custom_call_target="tpu_custom_call" | custom-call | tf_op jit(solution)/shard_map/pallas_call | solution.py:508
  39.6 3.8 %shard_map.87 = (f32[4,256,256]{2,1,0:T(8,128)}, f32[4,256,256]{2,1,0:T(8,128)}) custom-call(f32[4,256,256]{2,1,0:T(8,128)} %get-tuple-element.5.kap_in, bf16[4,256,256]{2,1,0:T(8,128)(2,1)} %get-tuple-element.6.high_in, bf16[4,256,256]{2,1,0:T(8,128)(2,1)} %get-tuple-element.7.low_in, bf16[256,256]{1,0:T(8,128)(2,1)} %constant.8.clone.th_in, ...), custom_call_target="tpu_custom_call" | custom-call | tf_op jit(solution)/shard_map/pallas_call | solution.py:527

commit v5 on v4

--- a/solution.py
+++ b/solution.py
@@ -70,11 +70,11 @@
 
 def kernel(
     frac_in, dir_in, div_in, th_in, tl_in, ratio_in, weight_in,
-    kap_out, high_out, low_out,
-    fx, dirs, divs, th, tl, ratio, weight,
-    axc, axd, axs, ayc, ayd, ays, kap, shi, slo, spec, mhi, mlo,
+    kap, inner_high, inner_low, th, tl,
+    fx, dirs, divs, ratio, weight,
+    axc, axd, axs, ayc, ayd, ays, shi, slo, fhi, flo, spec,
     lus, rc, pu, ru, od, rd, sd, ab,
-    in_sem, out_sem, fs_sem, fr_sem, c_sem, u_sem, round_sem,
+    in_sem, fs_sem, fr_sem, c_sem, u_sem, round_sem,
 ):
     me = lax.axis_index("gz")
     core = lax.rem(me, 2)
@@ -229,10 +229,13 @@
         scale = jnp.where(exists, 0.5 * TENSION, 0.0)
         store(outer, scale * kap[t] * (fx[t + 3] - fx[outer + 3]))
 
-    def transform(t):
-        inner = mm3(shi[t + 1], slo[t + 1], th[...], tl[...])
-        ih, il = split(inner)
-        spec[t + 1] = mm3(th[...], tl[...], ih, il)
+    def first_stage(planes):
+        for t in planes:
+            fhi[t + 1], flo[t + 1] = split(mm3(shi[t + 1], slo[t + 1], th[...], tl[...]))
+
+    def second_stage(planes, rows):
+        for t in planes:
+            spec[t + 1, rows, :] = mm3(th[rows, :], tl[rows, :], fhi[t + 1], flo[t + 1])
 
     near = 3 - 3 * core
     step = 2 * core - 1
@@ -266,7 +269,6 @@
     for load in loads[2:]:
         load.wait()
     beyond(near, near_halo, True)
-    transform(near_halo)
     pl.semaphore_wait(round_sem.at[1], len(y_ring))
     hail(2, z_ring)
     wait_far(0)
@@ -274,21 +276,22 @@
     flat_bend(place(3))
     upright_bend(place(1))
     source(near)
-    transform(near)
     wait_far(1)
     upright_bend(place(2))
     source(place(1))
-    transform(place(1))
+    early = (near_halo, near, place(1))
+    first_stage(early)
+    second_stage(early, slice(None))
     wait_far(2)
     upright_bend(place(3))
-    out_kap = pltpu.make_async_copy(kap, kap_out, out_sem.at[0])
-    out_kap.start()
     beyond(place(3), far_halo, has_cross)
     source(place(2))
     source(place(3))
-    transform(place(2))
-    transform(place(3))
-    transform(far_halo)
+    late = (place(2), place(3), far_halo)
+    first_stage(late)
+
+    def half_rows(half):
+        return pl.ds(pl.multiple_of(half * 128, 128), 128)
 
     def sums(half, i):
         rows = pl.ds(pl.multiple_of(half * 128 + i * ROWS, ROWS), ROWS)
@@ -302,24 +305,28 @@
         high = r * high + f[0]
         return low, high
 
+    second_stage(late, half_rows(1 - core))
+
     def sums_out(i, carry):
         rows = pl.ds(pl.multiple_of(i * ROWS, ROWS), ROWS)
         lus[0, rows, :], lus[1, rows, :] = sums(1 - core, i)
         return carry
 
-    lax.fori_loop(0, 4, sums_out, 0)
+    lax.fori_loop(0, 4, sums_out, 0, unroll=True)
     send_c = pltpu.make_async_remote_copy(
         src_ref=lus, dst_ref=rc.at[core], send_sem=c_sem.at[0], recv_sem=c_sem.at[1],
         device_id=(sibling,), device_id_type=MESH,
     )
     send_c.start()
 
+    second_stage(late, half_rows(core))
+
     def sums_own(i, carry):
         rows = pl.ds(pl.multiple_of(i * ROWS, ROWS), ROWS)
         rc[core, 0, rows, :], rc[core, 1, rows, :] = sums(core, i)
         return carry
 
-    lax.fori_loop(0, 4, sums_own, 0)
+    lax.fori_loop(0, 4, sums_own, 0, unroll=True)
     send_c.wait_recv()
 
     def power4(x):
@@ -434,20 +441,20 @@
                 rising.append(r * rising[t - 1] + f[t + 1])
             falling = ab[half, 1, local, :] + r * f[SLAB + 1]
             for t in range(SLAB - 1, -1, -1):
-                mhi[t, rows, :], mlo[t, rows, :] = split(w * (rising[t] + falling))
+                shi[t, rows, :], slo[t, rows, :] = split(w * (rising[t] + falling))
                 falling = r * (falling + f[t + 1])
             return carry
 
-        lax.fori_loop(0, 4, body, 0, unroll=2)
+        lax.fori_loop(0, 4, body, 0, unroll=True)
+        rows = half_rows(half)
+        for t in range(SLAB):
+            inner_high[t, rows, :], inner_low[t, rows, :] = split(
+                mm3(shi[t, rows, :], slo[t, rows, :], th[...], tl[...])
+            )
 
     modal(core)
     send_d.wait_recv()
     modal(1 - core)
-
-    out_high = pltpu.make_async_copy(mhi, high_out, out_sem.at[1])
-    out_low = pltpu.make_async_copy(mlo, low_out, out_sem.at[2])
-    out_high.start()
-    out_low.start()
 
     @pl.when(has_above)
     def _():
@@ -463,30 +470,15 @@
     send_d.wait_send()
     wait_parts(0, 0)
     wait_parts(1, 0)
-    out_kap.wait()
-    out_high.wait()
-    out_low.wait()
-
-
-def finish(kap_in, high_in, low_in, th_in, tl_in, kap_out, pre_out, kap, mhi, mlo, th, tl, pre, sem):
-    loads = [
-        pltpu.make_async_copy(source, target, sem.at[1 + i])
-        for i, (source, target) in enumerate(((th_in, th), (tl_in, tl), (high_in, mhi), (low_in, mlo)))
-    ]
-    fetch = pltpu.make_async_copy(kap_in, kap, sem.at[0])
-    passing = pltpu.make_async_copy(kap, kap_out, sem.at[9])
-    for load in loads:
-        load.start()
-    fetch.start()
-    for load in loads:
-        load.wait()
-    fetch.wait()
+
+
+def finish(kap, high, low, th, tl, kap_out, pre_out, pre, sem):
+    passing = pltpu.make_async_copy(kap, kap_out, sem.at[SLAB])
     passing.start()
     stores = []
     for t in range(SLAB):
-        ih, il = split(mm3(mhi[t], mlo[t], th[...], tl[...]))
-        pre[t] = mm3(th[...], tl[...], ih, il)
-        stores.append(pltpu.make_async_copy(pre.at[t], pre_out.at[t], sem.at[5 + t]))
+        pre[t] = mm3(th[...], tl[...], high[t], low[t])
+        stores.append(pltpu.make_async_copy(pre.at[t], pre_out.at[t], sem.at[t]))
         stores[t].start()
     passing.wait()
     for copy in stores:
@@ -497,43 +489,47 @@
     shape = (SLAB, SIZE, SIZE)
     plane = (SIZE, SIZE)
     high, low, ratio, weight = tables()
-    anywhere = pl.BlockSpec(memory_space=pl.ANY)
+    far = pl.BlockSpec(memory_space=pltpu.HBM)
     vm = pltpu.VMEM
+    close = pl.BlockSpec(memory_space=vm)
     dma = pltpu.SemaphoreType.DMA
-    high, low = jnp.asarray(high), jnp.asarray(low)
     whole = jax.ShapeDtypeStruct(shape, F32)
     half = jax.ShapeDtypeStruct(shape, BF16)
-    params = dict(vmem_limit_bytes=56 * 1024 * 1024)
+    table = jax.ShapeDtypeStruct(plane, BF16)
+    params = dict(vmem_limit_bytes=40 * 1024 * 1024)
     six = vm((SLAB + 2,) + plane, F32)
-    curvature, modal_high, modal_low = pl.pallas_call(
+    six_half = vm((SLAB + 2,) + plane, BF16)
+    inputs = (
+        fraction, column_dir, divergence, jnp.asarray(high), jnp.asarray(low), jnp.asarray(ratio), jnp.asarray(weight),
+    )
+    handed_on = pl.pallas_call(
         kernel,
-        out_shape=(whole, half, half),
-        in_specs=[anywhere] * 7,
-        out_specs=(anywhere,) * 3,
+        out_shape=(whole, half, half, table, table),
+        in_specs=[far] * 7,
+        out_specs=(close,) * 5,
         scratch_shapes=[
             vm((10,) + plane, F32), vm(shape, jnp.int32), vm(shape, F32),
-            vm(plane, BF16), vm(plane, BF16), vm(plane, F32), vm(plane, F32),
+            vm(plane, F32), vm(plane, F32),
             six, six, six, six, six, six,
-            vm(shape, F32), vm((SLAB + 2,) + plane, BF16), vm((SLAB + 2,) + plane, BF16), six,
-            vm(shape, BF16), vm(shape, BF16),
+            six_half, six_half, six_half, six_half, six,
             vm((2, 128, SIZE), F32), vm((2, 2, 128, SIZE), F32),
             vm((CHIPS, 8, 128), F32), vm((CHIPS, 8, 128), F32),
             vm((CHIPS, 8, 128), F32), vm((CHIPS, 8, 128), F32),
             vm((2, 128, SIZE), F32), vm((2, 2, 128, SIZE), F32),
-            dma((7,)), dma((3,)), dma((2, 3)), dma((2, 3)), dma((4,)), dma((2, 2)), pltpu.SemaphoreType.REGULAR((3,)),
+            dma((7,)), dma((2, 3)), dma((2, 3)), dma((4,)), dma((2, 2)), pltpu.SemaphoreType.REGULAR((3,)),
         ],
         compiler_params=pltpu.CompilerParams(collective_id=0, has_side_effects=True, **params),
-    )(fraction, column_dir, divergence, high, low, jnp.asarray(ratio), jnp.asarray(weight))
+    )(*(pltpu.with_memory_space_constraint(value, pltpu.HBM) for value in inputs))
     return pl.pallas_call(
         finish,
         out_shape=(whole, whole),
-        in_specs=[anywhere] * 5,
-        out_specs=(anywhere,) * 2,
+        in_specs=[close] * 5,
+        out_specs=(far,) * 2,
         scratch_shapes=[
-            vm(shape, F32), vm(shape, BF16), vm(shape, BF16), vm(plane, BF16), vm(plane, BF16), vm(shape, F32), dma((10,)),
+            vm(shape, F32), dma((SLAB + 1,)),
         ],
         compiler_params=pltpu.CompilerParams(**params),
-    )(curvature, modal_high, modal_low, high, low)
+    )(*handed_on)
 
 
 def solution(mesh):

time: 43.5 us -> 40.5 us (0.931)
  Pallas kernels: 42.8 us -> 39.7 us
    pallas_call x2, Pallas kernels: 42.8 us -> 39.7 us  [the longest x1 38.3 us: shards(): pl.pallas_call(kernel, out_shape=(whole, half, half, table, table), in_sp...]
where the time goes in v5:
time: 40.5 us; the launch traced here: 40.4 us
  Pallas kernels  39.7 us (98%)
  between operations  0.64 us (2%)
    pallas_call x1, Pallas kernels, shards(): pl.pallas_call(kernel, out_shape=(whole, half, half, table, table), in_sp...  38.3 us
    pallas_call x1, Pallas kernels, shards(): pl.pallas_call(finish, out_shape=(whole, whole), in_specs=[close] * 5, ou...  1.41 us

profile of v5, /device:TPU:1, one launch (start us, length us, event | category | flops | bytes accessed | tf_op | source)
XLA Modules:
  0.0 40.4 jit_solution(14476104937896162571)
XLA Ops:
  0.6 38.3 %shard_map.86 = (f32[4,256,256]{2,1,0:T(8,128)S(1)}, bf16[4,256,256]{2,1,0:T(8,128)(2,1)S(1)}, bf16[4,256,256]{2,1,0:T(8,128)(2,1)S(1)}, bf16[256,256]{1,0:T(8,128)(2,1)S(1)}, bf16[256,256]{1,0:T(8,128)(2,1)S(1)}) custom-call(f32[4,256,256]{2,1,0:T(8,128)} %frac_in.1, s32[4,256,256]{2,1,0:T(8,128)} %dir_in.1, f32[4,256,256]{2,1,0:T(8,128)} %div_in.1, ...), custom_call_target="tpu_custom_call" | custom-call | tf_op jit(solution)/shard_map/pallas_call | solution.py:505
  39.0 1.4 %shard_map.87 = (f32[4,256,256]{2,1,0:T(8,128)}, f32[4,256,256]{2,1,0:T(8,128)}) custom-call(f32[4,256,256]{2,1,0:T(8,128)S(1)} %get-tuple-element.7.kap, bf16[4,256,256]{2,1,0:T(8,128)(2,1)S(1)} %get-tuple-element.8.high, bf16[4,256,256]{2,1,0:T(8,128)(2,1)S(1)} %get-tuple-element.9.low, bf16[256,256]{1,0:T(8,128)(2,1)S(1)} %get-tuple-element.10.th, ...), custom_call_target="tpu_custom_call" | custom-call | tf_op jit(solution)/shard_map/pallas_call | solution.py:523

commit v6 on v5

--- a/solution.py
+++ b/solution.py
@@ -14,6 +14,9 @@
 DEVICES = 128
 CHIPS = 64
 ROWS = 32
+PIECES = ((0, 80), (80, 144), (144, 208), (208, 256))
+BENT = ((8, 72), (72, 136), (136, 200), (200, 264))
+FED = ((16, 64), (64, 128), (128, 192), (192, 272))
 MESH = pl.DeviceIdType.MESH
 F32 = jnp.float32
 BF16 = jnp.bfloat16
@@ -72,7 +75,7 @@
     frac_in, dir_in, div_in, th_in, tl_in, ratio_in, weight_in,
     kap, inner_high, inner_low, th, tl,
     fx, dirs, divs, ratio, weight,
-    axc, axd, axs, ayc, ayd, ays, shi, slo, fhi, flo, spec,
+    axc, axd, axs, ayc, ayd, ays, shi, slo, fhi, flo, spec, part, heights,
     lus, rc, pu, ru, od, rd, sd, ab,
     in_sem, fs_sem, fr_sem, c_sem, u_sem, round_sem,
 ):
@@ -99,6 +102,19 @@
     y_ring = chips_at([(0, 2, 0), (0, 1, 0), (0, 3, 0)])
     z_ring = chips_at([(2, 0, 0), (1, 0, 0), (3, 0, 0)])
 
+    barrier = pltpu.get_barrier_semaphore()
+
+    def greet(target):
+        pl.semaphore_signal(barrier, inc=1, device_id=(target,), device_id_type=MESH)
+
+    @pl.when(has_cross)
+    def _():
+        greet(cross)
+
+    greet(sibling)
+    for other in nearest:
+        greet(2 * other + core)
+
     loads = [
         pltpu.make_async_copy(frac_in, fx.at[pl.ds(3, SLAB)], in_sem.at[0]),
         pltpu.make_async_copy(dir_in, dirs, in_sem.at[1]),
@@ -111,20 +127,6 @@
     for load in loads:
         load.start()
 
-    barrier = pltpu.get_barrier_semaphore()
-
-    def greet(target):
-        pl.semaphore_signal(barrier, inc=1, device_id=(target,), device_id_type=MESH)
-
-    greet(sibling)
-
-    @pl.when(has_cross)
-    def _():
-        greet(cross)
-
-    for other in nearest:
-        greet(2 * other + core)
-
     peers = 1 + len(nearest)
     pl.semaphore_wait(barrier, jnp.where(has_cross, peers + 1, peers))
 
@@ -134,27 +136,37 @@
                 round_sem.at[i], inc=1, device_id=(2 * other + core,), device_id_type=MESH
             )
 
-    def frac_above(j):
-        return pltpu.make_async_remote_copy(
-            src_ref=frac_in.at[3 - j], dst_ref=fx.at[2 - j], send_sem=fs_sem.at[0, j],
-            recv_sem=fr_sem.at[0, j], device_id=(me + 1,), device_id_type=MESH,
-        )
-
-    def frac_below(j):
-        return pltpu.make_async_remote_copy(
-            src_ref=frac_in.at[j], dst_ref=fx.at[7 + j], send_sem=fs_sem.at[1, j],
-            recv_sem=fr_sem.at[1, j], device_id=(me - 1,), device_id_type=MESH,
-        )
-
-    @pl.when(has_above)
-    def _():
-        for j in range(3):
-            frac_above(j).start()
-
-    @pl.when(has_below)
-    def _():
-        for j in range(3):
-            frac_below(j).start()
+    def halo_copies(side):
+        for piece in range(2 + len(PIECES)):
+            j = min(piece, 2)
+            first, last = (0, SIZE) if piece < 2 else PIECES[piece - 2]
+            rows = pl.ds(first, last - first)
+            source, target = (3 - j, 2 - j) if side == 0 else (j, 7 + j)
+            yield pltpu.make_async_remote_copy(
+                src_ref=frac_in.at[source, rows], dst_ref=fx.at[target, rows],
+                send_sem=fs_sem.at[side, piece], recv_sem=fr_sem.at[side, piece],
+                device_id=(me + 1 - 2 * side,), device_id_type=MESH,
+            )
+
+    def send_halo(side):
+        for copy in halo_copies(side):
+            copy.start()
+
+    @pl.when(jnp.logical_and(core == 0, has_below))
+    def _():
+        send_halo(1)
+
+    @pl.when(core == 0)
+    def _():
+        send_halo(0)
+
+    @pl.when(jnp.logical_and(core == 1, has_above))
+    def _():
+        send_halo(0)
+
+    @pl.when(core == 1)
+    def _():
+        send_halo(1)
 
     hail(0, nearest)
     zero_plane = jnp.zeros((SIZE, SIZE), F32)
@@ -197,37 +209,59 @@
         s_at = pick(axs[t + 1], ays[t + 1])
         kap[t] = bend(hi - lo, d_at, hi + lo - 2.0 * at, s_at, d_hi - d_lo)
 
-    def upright_bend(t):
-        h = fx[t]
-        for j in range(1, 7):
-            h = h + fx[t + j]
+    def upright(h):
         right, left = up(h, 1), down(h, 1)
         db = right - left
         sb = right + left
         plus, minus = up(h, 0), down(h, 0)
         dab = up(db, 0) - down(db, 0)
-        value = bend(plus - minus, db, plus + minus - 2.0 * h, sb - 2.0 * h, dab)
+        return bend(plus - minus, db, plus + minus - 2.0 * h, sb - 2.0 * h, dab)
+
+    def upright_bend(t):
+        h = fx[t]
+        for j in range(1, 7):
+            h = h + fx[t + j]
+        value = upright(h)
         where = dirs[t]
         kap[t] = jnp.where(where == 0, value, jnp.where(where == 3, 0.0, kap[t]))
 
     def store(t, value):
         shi[t + 1], slo[t + 1] = split(value)
 
-    def source(t):
+    def source(t, hidden):
         f = fx[t + 3]
         k = kap[t]
         face = (k + up(k, 0)) * (up(f, 0) - f)
         total = face - down(face, 0)
         face = (k + up(k, 1)) * (up(f, 1) - f)
         total = total + face - down(face, 1)
-        above = jnp.where(t == SLAB - 1, 0.0, kap[jnp.minimum(t + 1, SLAB - 1)])
-        below = jnp.where(t == 0, 0.0, kap[jnp.maximum(t - 1, 0)])
-        total = total + (k + above) * (fx[t + 4] - f) - (k + below) * (f - fx[t + 2])
-        store(t, divs[t] + (0.5 * TENSION) * total)
-
-    def beyond(t, outer, exists):
-        scale = jnp.where(exists, 0.5 * TENSION, 0.0)
-        store(outer, scale * kap[t] * (fx[t + 3] - fx[outer + 3]))
+
+        def beside(other):
+            shown = jnp.logical_and(jnp.logical_and(other >= 0, other < SLAB), other != hidden)
+            return jnp.where(shown, kap[jnp.clip(other, 0, SLAB - 1)], 0.0)
+
+        total = total + (k + beside(t + 1)) * (fx[t + 4] - f) - (k + beside(t - 1)) * (f - fx[t + 2])
+        return divs[t] + (0.5 * TENSION) * total
+
+    def beyond(t, outer):
+        store(outer, (0.5 * TENSION) * kap[t] * (fx[t + 3] - fx[outer + 3]))
+
+    def ring(ref, t, first, last):
+        if first < 0:
+            return jnp.concatenate([ref[t, first + SIZE : SIZE], ref[t, 0:last]], axis=0)
+        if last > SIZE:
+            return jnp.concatenate([ref[t, first:SIZE], ref[t, 0 : last - SIZE]], axis=0)
+        return ref[t, first:last]
+
+    def put(ref, t, first, last, value):
+        if last > SIZE:
+            ref[t, first:SIZE] = value[: SIZE - first]
+            ref[t, 0 : last - SIZE] = value[SIZE - first :]
+        else:
+            ref[t, first:last] = value
+
+    def inner_rows(x):
+        return x[8 : x.shape[0] - 8]
 
     def first_stage(planes):
         for t in planes:
@@ -247,13 +281,15 @@
     near_halo = 4 - 5 * core
     far_halo = 5 * core - 1
 
-    def wait_frac(side, j):
-        pltpu.make_async_copy(frac_in.at[0], fx.at[0], fr_sem.at[side, j]).wait()
-
-    def wait_far(j):
+    def wait_frac(side, piece):
+        first, last = (0, SIZE) if piece < 2 else PIECES[piece - 2]
+        rows = pl.ds(first, last - first)
+        pltpu.make_async_copy(frac_in.at[0, rows], fx.at[0, rows], fr_sem.at[side, piece]).wait()
+
+    def wait_far(piece):
         @pl.when(has_cross)
         def _():
-            wait_frac(core, j)
+            wait_frac(core, piece)
 
     loads[0].wait()
     lax.fori_loop(0, SLAB, lambda t, c: (flat_heights(t), c)[1], 0)
@@ -261,34 +297,62 @@
     hail(1, y_ring)
     loads[1].wait()
     lax.fori_loop(1, 3, lambda t, c: (flat_bend(t), c)[1], 0)
-    for j in range(3):
-        wait_frac(near_side, j)
+    for piece in range(2 + len(PIECES)):
+        wait_frac(near_side, piece)
     flat_heights(near_halo)
     flat_bend(near)
     upright_bend(near)
     for load in loads[2:]:
         load.wait()
-    beyond(near, near_halo, True)
+    beyond(near, near_halo)
     pl.semaphore_wait(round_sem.at[1], len(y_ring))
     hail(2, z_ring)
     wait_far(0)
     flat_heights(far_halo)
     flat_bend(place(3))
     upright_bend(place(1))
-    source(near)
+    store(near, source(near, -1))
     wait_far(1)
     upright_bend(place(2))
-    source(place(1))
+    store(place(1), source(place(1), -1))
     early = (near_halo, near, place(1))
     first_stage(early)
     second_stage(early, slice(None))
-    wait_far(2)
-    upright_bend(place(3))
-    beyond(place(3), far_halo, has_cross)
-    source(place(2))
-    source(place(3))
-    late = (place(2), place(3), far_halo)
-    first_stage(late)
+    outer, third = place(3), place(2)
+    part[0] = source(third, outer)
+    summed = fx[1 + 2 * core]
+    for j in range(1, 6):
+        summed = summed + fx[1 + 2 * core + j]
+    heights[0] = summed
+    scale = jnp.where(has_cross, 0.5 * TENSION, 0.0)
+    late = (third, outer, far_halo)
+
+    for c in range(len(PIECES)):
+        wait_far(2 + c)
+        a, b = BENT[c]
+        h = ring(heights, 0, a - 8, b + 8) + ring(fx, 9 * core, a - 8, b + 8)
+        value = inner_rows(upright(h))
+        where = ring(dirs, outer, a, b)
+        flat = ring(kap, outer, a, b)
+        put(kap, outer, a, b, jnp.where(where == 0, value, jnp.where(where == 3, 0.0, flat)))
+        a, b = FED[c]
+        f, k = ring(fx, outer + 3, a - 8, b + 8), ring(kap, outer, a - 8, b + 8)
+        face = (k + up(k, 0)) * (up(f, 0) - f)
+        total = inner_rows(face - down(face, 0))
+        f, k = inner_rows(f), inner_rows(k)
+        face = (k + up(k, 1)) * (up(f, 1) - f)
+        total = total + face - down(face, 1)
+        f_third, f_halo = ring(fx, third + 3, a, b), ring(fx, far_halo + 3, a, b)
+        total = total + (ring(kap, third, a, b) + k) * (f_third - f) + k * (f_halo - f)
+        fed = (
+            ring(part, 0, a, b) + (0.5 * TENSION) * k * (f - f_third),
+            ring(divs, outer, a, b) + (0.5 * TENSION) * total,
+            scale * k * (f - f_halo),
+        )
+        for t, rows in zip(late, fed):
+            high, low = split(mm3(*split(rows), th[...], tl[...]))
+            put(fhi, t + 1, a, b, high)
+            put(flo, t + 1, a, b, low)
 
     def half_rows(half):
         return pl.ds(pl.multiple_of(half * 128, 128), 128)
@@ -307,27 +371,23 @@
 
     second_stage(late, half_rows(1 - core))
 
-    def sums_out(i, carry):
-        rows = pl.ds(pl.multiple_of(i * ROWS, ROWS), ROWS)
-        lus[0, rows, :], lus[1, rows, :] = sums(1 - core, i)
-        return carry
-
-    lax.fori_loop(0, 4, sums_out, 0, unroll=True)
-    send_c = pltpu.make_async_remote_copy(
-        src_ref=lus, dst_ref=rc.at[core], send_sem=c_sem.at[0], recv_sem=c_sem.at[1],
-        device_id=(sibling,), device_id_type=MESH,
-    )
-    send_c.start()
+    def give(q):
+        rows = pl.ds(64 * q, 64)
+        return pltpu.make_async_remote_copy(
+            src_ref=lus.at[:, rows], dst_ref=rc.at[core, :, rows], send_sem=c_sem.at[0, q], recv_sem=c_sem.at[1, q],
+            device_id=(sibling,), device_id_type=MESH,
+        )
+
+    for q in range(2):
+        for i in (2 * q, 2 * q + 1):
+            rows = pl.ds(i * ROWS, ROWS)
+            lus[0, rows, :], lus[1, rows, :] = sums(1 - core, i)
+        give(q).start()
 
     second_stage(late, half_rows(core))
-
-    def sums_own(i, carry):
-        rows = pl.ds(pl.multiple_of(i * ROWS, ROWS), ROWS)
+    for i in range(4):
+        rows = pl.ds(i * ROWS, ROWS)
         rc[core, 0, rows, :], rc[core, 1, rows, :] = sums(core, i)
-        return carry
-
-    lax.fori_loop(0, 4, sums_own, 0, unroll=True)
-    send_c.wait_recv()
 
     def power4(x):
         x = x * x
@@ -350,7 +410,9 @@
             pu[i * 4 + lane * 2 + 1] = jnp.where(first_half, swap(lt), ut)
         return carry
 
-    lax.fori_loop(0, 16, cut, 0, unroll=4)
+    for q in range(2):
+        give(q).wait_recv()
+        lax.fori_loop(8 * q, 8 * q + 8, cut, 0, unroll=True)
 
     def send_part(other, level, source_ref, target_ref):
         return pltpu.make_async_remote_copy(
@@ -422,12 +484,16 @@
         sd[1, rows, :] = jnp.where(even, b, b_far)
         return carry
 
-    lax.fori_loop(0, 16, spread, 0, unroll=4)
-    send_d = pltpu.make_async_remote_copy(
-        src_ref=sd, dst_ref=ab.at[core], send_sem=c_sem.at[2], recv_sem=c_sem.at[3],
-        device_id=(sibling,), device_id_type=MESH,
-    )
-    send_d.start()
+    def hand(q):
+        rows = pl.ds(64 * q, 64)
+        return pltpu.make_async_remote_copy(
+            src_ref=sd.at[:, rows], dst_ref=ab.at[core, :, rows], send_sem=c_sem.at[2, q], recv_sem=c_sem.at[3, q],
+            device_id=(sibling,), device_id_type=MESH,
+        )
+
+    for q in range(2):
+        lax.fori_loop(8 * q, 8 * q + 8, spread, 0, unroll=True)
+        hand(q).start()
 
     def modal(half):
         def body(i, carry):
@@ -453,21 +519,23 @@
             )
 
     modal(core)
-    send_d.wait_recv()
+    for q in range(2):
+        hand(q).wait_recv()
     modal(1 - core)
 
     @pl.when(has_above)
     def _():
-        for j in range(3):
-            frac_above(j).wait_send()
+        for copy in halo_copies(0):
+            copy.wait_send()
 
     @pl.when(has_below)
     def _():
-        for j in range(3):
-            frac_below(j).wait_send()
-
-    send_c.wait_send()
-    send_d.wait_send()
+        for copy in halo_copies(1):
+            copy.wait_send()
+
+    for q in range(2):
+        give(q).wait_send()
+        hand(q).wait_send()
     wait_parts(0, 0)
     wait_parts(1, 0)
 
@@ -512,11 +580,12 @@
             vm(plane, F32), vm(plane, F32),
             six, six, six, six, six, six,
             six_half, six_half, six_half, six_half, six,
+            vm((1,) + plane, F32), vm((1,) + plane, F32),
             vm((2, 128, SIZE), F32), vm((2, 2, 128, SIZE), F32),
             vm((CHIPS, 8, 128), F32), vm((CHIPS, 8, 128), F32),
             vm((CHIPS, 8, 128), F32), vm((CHIPS, 8, 128), F32),
             vm((2, 128, SIZE), F32), vm((2, 2, 128, SIZE), F32),
-            dma((7,)), dma((2, 3)), dma((2, 3)), dma((4,)), dma((2, 2)), pltpu.SemaphoreType.REGULAR((3,)),
+            dma((7,)), dma((2, 6)), dma((2, 6)), dma((4, 2)), dma((2, 2)), pltpu.SemaphoreType.REGULAR((3,)),
         ],
         compiler_params=pltpu.CompilerParams(collective_id=0, has_side_effects=True, **params),
     )(*(pltpu.with_memory_space_constraint(value, pltpu.HBM) for value in inputs))

time: 40.5 us -> 40.1 us (level)
  no operation moved by 1% of the time
where the time goes in v6:
time: 40.1 us; the launch traced here: 40 us
  Pallas kernels  39.4 us (98%)
  between operations  0.64 us (2%)
    pallas_call x1, Pallas kernels, shards(): pl.pallas_call(kernel, out_shape=(whole, half, half, table, table), in_sp...  38 us
    pallas_call x1, Pallas kernels, shards(): pl.pallas_call(finish, out_shape=(whole, whole), in_specs=[close] * 5, ou...  1.41 us

profile of v6, /device:TPU:1, one launch (start us, length us, event | category | flops | bytes accessed | tf_op | source)
XLA Modules:
  0.0 40.0 jit_solution(11737297526941231229)
XLA Ops:
  0.6 38.0 %shard_map.86 = (f32[4,256,256]{2,1,0:T(8,128)S(1)}, bf16[4,256,256]{2,1,0:T(8,128)(2,1)S(1)}, bf16[4,256,256]{2,1,0:T(8,128)(2,1)S(1)}, bf16[256,256]{1,0:T(8,128)(2,1)S(1)}, bf16[256,256]{1,0:T(8,128)(2,1)S(1)}) custom-call(f32[4,256,256]{2,1,0:T(8,128)} %frac_in.1, s32[4,256,256]{2,1,0:T(8,128)} %dir_in.1, f32[4,256,256]{2,1,0:T(8,128)} %div_in.1, ...), custom_call_target="tpu_custom_call" | custom-call | tf_op jit(solution)/shard_map/pallas_call | solution.py:573
  38.6 1.4 %shard_map.87 = (f32[4,256,256]{2,1,0:T(8,128)}, f32[4,256,256]{2,1,0:T(8,128)}) custom-call(f32[4,256,256]{2,1,0:T(8,128)S(1)} %get-tuple-element.7.kap, bf16[4,256,256]{2,1,0:T(8,128)(2,1)S(1)} %get-tuple-element.8.high, bf16[4,256,256]{2,1,0:T(8,128)(2,1)S(1)} %get-tuple-element.9.low, bf16[256,256]{1,0:T(8,128)(2,1)S(1)} %get-tuple-element.10.th, ...), custom_call_target="tpu_custom_call" | custom-call | tf_op jit(solution)/shard_map/pallas_call | solution.py:592

commit v7 on v6

--- a/solution.py
+++ b/solution.py
@@ -14,9 +14,9 @@
 DEVICES = 128
 CHIPS = 64
 ROWS = 32
-PIECES = ((0, 80), (80, 144), (144, 208), (208, 256))
-BENT = ((8, 72), (72, 136), (136, 200), (200, 264))
-FED = ((16, 64), (64, 128), (128, 192), (192, 272))
+PIECES = ((0, 96), (96, 192), (192, 256))
+BENT = ((8, 88), (88, 184), (184, 264))
+FED = ((16, 80), (80, 176), (176, 272))
 MESH = pl.DeviceIdType.MESH
 F32 = jnp.float32
 BF16 = jnp.bfloat16
@@ -312,23 +312,25 @@
     flat_bend(place(3))
     upright_bend(place(1))
     store(near, source(near, -1))
+    second = place(1)
+    part[1] = source(second, place(2))
+    first_stage((near_halo, near))
+    second_stage((near_halo, near), slice(None))
     wait_far(1)
     upright_bend(place(2))
-    store(place(1), source(place(1), -1))
-    early = (near_halo, near, place(1))
-    first_stage(early)
-    second_stage(early, slice(None))
+    store(second, part[1] + (0.5 * TENSION) * kap[place(2)] * (fx[place(2) + 3] - fx[second + 3]))
     outer, third = place(3), place(2)
-    part[0] = source(third, outer)
-    summed = fx[1 + 2 * core]
-    for j in range(1, 6):
-        summed = summed + fx[1 + 2 * core + j]
-    heights[0] = summed
-    scale = jnp.where(has_cross, 0.5 * TENSION, 0.0)
     late = (third, outer, far_halo)
 
-    for c in range(len(PIECES)):
-        wait_far(2 + c)
+    def prepare():
+        part[0] = source(third, outer)
+        summed = fx[1 + 2 * core]
+        for j in range(1, 6):
+            summed = summed + fx[1 + 2 * core + j]
+        heights[0] = summed
+
+    def late_piece(c):
+        scale = jnp.where(has_cross, 0.5 * TENSION, 0.0)
         a, b = BENT[c]
         h = ring(heights, 0, a - 8, b + 8) + ring(fx, 9 * core, a - 8, b + 8)
         value = inner_rows(upright(h))
@@ -349,10 +351,18 @@
             ring(divs, outer, a, b) + (0.5 * TENSION) * total,
             scale * k * (f - f_halo),
         )
-        for t, rows in zip(late, fed):
-            high, low = split(mm3(*split(rows), th[...], tl[...]))
-            put(fhi, t + 1, a, b, high)
-            put(flo, t + 1, a, b, low)
+        high, low = split(mm3(*split(jnp.concatenate(fed, axis=0)), th[...], tl[...]))
+        for n, t in enumerate(late):
+            rows = slice(n * (b - a), (n + 1) * (b - a))
+            put(fhi, t + 1, a, b, high[rows])
+            put(flo, t + 1, a, b, low[rows])
+
+    prepare()
+    for c in range(len(PIECES)):
+        wait_far(2 + c)
+        late_piece(c)
+        if c == 0:
+            first_stage((second,))
 
     def half_rows(half):
         return pl.ds(pl.multiple_of(half * 128, 128), 128)
@@ -369,7 +379,7 @@
         high = r * high + f[0]
         return low, high
 
-    second_stage(late, half_rows(1 - core))
+    second_stage((second,) + late, half_rows(1 - core))
 
     def give(q):
         rows = pl.ds(64 * q, 64)
@@ -384,7 +394,7 @@
             lus[0, rows, :], lus[1, rows, :] = sums(1 - core, i)
         give(q).start()
 
-    second_stage(late, half_rows(core))
+    second_stage((second,) + late, half_rows(core))
     for i in range(4):
         rows = pl.ds(i * ROWS, ROWS)
         rc[core, 0, rows, :], rc[core, 1, rows, :] = sums(core, i)
@@ -580,12 +590,12 @@
             vm(plane, F32), vm(plane, F32),
             six, six, six, six, six, six,
             six_half, six_half, six_half, six_half, six,
-            vm((1,) + plane, F32), vm((1,) + plane, F32),
+            vm((2,) + plane, F32), vm((1,) + plane, F32),
             vm((2, 128, SIZE), F32), vm((2, 2, 128, SIZE), F32),
             vm((CHIPS, 8, 128), F32), vm((CHIPS, 8, 128), F32),
             vm((CHIPS, 8, 128), F32), vm((CHIPS, 8, 128), F32),
             vm((2, 128, SIZE), F32), vm((2, 2, 128, SIZE), F32),
-            dma((7,)), dma((2, 6)), dma((2, 6)), dma((4, 2)), dma((2, 2)), pltpu.SemaphoreType.REGULAR((3,)),
+            dma((7,)), dma((2, 5)), dma((2, 5)), dma((4, 2)), dma((2, 2)), pltpu.SemaphoreType.REGULAR((3,)),
         ],
         compiler_params=pltpu.CompilerParams(collective_id=0, has_side_effects=True, **params),
     )(*(pltpu.with_memory_space_constraint(value, pltpu.HBM) for value in inputs))

time: 40.1 us -> 39.3 us (0.980)
  Pallas kernels: 39.4 us -> 38.5 us
    pallas_call x1, Pallas kernels: 38 us -> 37.1 us  [shards(): pl.pallas_call(kernel, out_shape=(whole, half, half, table, table), in_sp...]
where the time goes in v7:
time: 39.3 us; the launch traced here: 39.1 us
  Pallas kernels  38.5 us (98%)
  between operations  0.64 us (2%)
    pallas_call x1, Pallas kernels, shards(): pl.pallas_call(kernel, out_shape=(whole, half, half, table, table), in_sp...  37.1 us
    pallas_call x1, Pallas kernels, shards(): pl.pallas_call(finish, out_shape=(whole, whole), in_specs=[close] * 5, ou...  1.41 us

profile of v7, /device:TPU:1, one launch (start us, length us, event | category | flops | bytes accessed | tf_op | source)
XLA Modules:
  0.0 39.1 jit_solution(8508275027311127681)
XLA Ops:
  0.6 37.1 %shard_map.86 = (f32[4,256,256]{2,1,0:T(8,128)S(1)}, bf16[4,256,256]{2,1,0:T(8,128)(2,1)S(1)}, bf16[4,256,256]{2,1,0:T(8,128)(2,1)S(1)}, bf16[256,256]{1,0:T(8,128)(2,1)S(1)}, bf16[256,256]{1,0:T(8,128)(2,1)S(1)}) custom-call(f32[4,256,256]{2,1,0:T(8,128)} %frac_in.1, s32[4,256,256]{2,1,0:T(8,128)} %dir_in.1, f32[4,256,256]{2,1,0:T(8,128)} %div_in.1, ...), custom_call_target="tpu_custom_call" | custom-call | tf_op jit(solution)/shard_map/pallas_call | solution.py:583
  37.7 1.4 %shard_map.87 = (f32[4,256,256]{2,1,0:T(8,128)}, f32[4,256,256]{2,1,0:T(8,128)}) custom-call(f32[4,256,256]{2,1,0:T(8,128)S(1)} %get-tuple-element.7.kap, bf16[4,256,256]{2,1,0:T(8,128)(2,1)S(1)} %get-tuple-element.8.high, bf16[4,256,256]{2,1,0:T(8,128)(2,1)S(1)} %get-tuple-element.9.low, bf16[256,256]{1,0:T(8,128)(2,1)S(1)} %get-tuple-element.10.th, ...), custom_call_target="tpu_custom_call" | custom-call | tf_op jit(solution)/shard_map/pallas_call | solution.py:602

commit v8 on v7

--- a/solution.py
+++ b/solution.py
@@ -363,6 +363,8 @@
         late_piece(c)
         if c == 0:
             first_stage((second,))
+        if c == 1:
+            second_stage((second,), slice(None))
 
     def half_rows(half):
         return pl.ds(pl.multiple_of(half * 128, 128), 128)
@@ -379,7 +381,7 @@
         high = r * high + f[0]
         return low, high
 
-    second_stage((second,) + late, half_rows(1 - core))
+    second_stage(late, half_rows(1 - core))
 
     def give(q):
         rows = pl.ds(64 * q, 64)
@@ -394,7 +396,7 @@
             lus[0, rows, :], lus[1, rows, :] = sums(1 - core, i)
         give(q).start()
 
-    second_stage((second,) + late, half_rows(core))
+    second_stage(late, half_rows(core))
     for i in range(4):
         rows = pl.ds(i * ROWS, ROWS)
         rc[core, 0, rows, :], rc[core, 1, rows, :] = sums(core, i)
@@ -438,8 +440,6 @@
     for other in others:
         send_part(other, 0, pu, ru).start()
     ru[chip] = pu[chip]
-    wait_parts(0, 1)
-
     tile_row = lax.div(chip, 4)
     tile_lane = lax.rem(lax.div(chip, 2), 2)
     tile_half = lax.rem(chip, 2)
@@ -452,6 +452,9 @@
     r8 = power4(rt * rt)
     r64 = power4(r8 * r8)
     r513 = power4(r64 * r64) * rt
+    settle = 1.0 / (1.0 - r513 * r513)
+    wait_parts(0, 1)
+
     merged = [jnp.where(first_half, ru[j], ru[CHIPS - 1 - j]) for j in range(CHIPS)]
     blocks = []
     for b in range(8):
@@ -462,7 +465,7 @@
     ends = blocks[0]
     for b in range(1, 8):
         ends = r64 * ends + blocks[b]
-    walls = (swap(ends) - r513 * ends) / (1.0 - r513 * r513)
+    walls = (swap(ends) - r513 * ends) * settle
     starts = [-(rt * walls)]
     for b in range(7):
         starts.append(r64 * starts[b] + blocks[b])
@@ -505,33 +508,30 @@
         lax.fori_loop(8 * q, 8 * q + 8, spread, 0, unroll=True)
         hand(q).start()
 
-    def modal(half):
-        def body(i, carry):
-            local = pl.ds(pl.multiple_of(i * ROWS, ROWS), ROWS)
-            rows = pl.ds(pl.multiple_of(half * 128 + i * ROWS, ROWS), ROWS)
-            r = ratio[rows, :]
-            w = weight[rows, :]
-            f = [spec[t, rows, :] for t in range(SLAB + 2)]
-            rising = [r * f[0] + ab[half, 0, local, :] + f[1]]
-            for t in range(1, SLAB):
-                rising.append(r * rising[t - 1] + f[t + 1])
-            falling = ab[half, 1, local, :] + r * f[SLAB + 1]
-            for t in range(SLAB - 1, -1, -1):
-                shi[t, rows, :], slo[t, rows, :] = split(w * (rising[t] + falling))
-                falling = r * (falling + f[t + 1])
-            return carry
-
-        lax.fori_loop(0, 4, body, 0, unroll=True)
-        rows = half_rows(half)
+    def modal(half, q):
+        local = pl.ds(64 * q, 64)
+        rows = pl.ds(pl.multiple_of(half * 128 + 64 * q, 64), 64)
+        r = ratio[rows, :]
+        w = weight[rows, :]
+        f = [spec[t, rows, :] for t in range(SLAB + 2)]
+        rising = [r * f[0] + ab[half, 0, local, :] + f[1]]
+        for t in range(1, SLAB):
+            rising.append(r * rising[t - 1] + f[t + 1])
+        falling = ab[half, 1, local, :] + r * f[SLAB + 1]
+        values = [None] * SLAB
+        for t in range(SLAB - 1, -1, -1):
+            values[t] = w * (rising[t] + falling)
+            falling = r * (falling + f[t + 1])
+        high, low = split(mm3(*split(jnp.concatenate(values, axis=0)), th[...], tl[...]))
         for t in range(SLAB):
-            inner_high[t, rows, :], inner_low[t, rows, :] = split(
-                mm3(shi[t, rows, :], slo[t, rows, :], th[...], tl[...])
-            )
-
-    modal(core)
+            inner_high[t, rows, :] = high[64 * t : 64 * t + 64]
+            inner_low[t, rows, :] = low[64 * t : 64 * t + 64]
+
+    for q in range(2):
+        modal(core, q)
     for q in range(2):
         hand(q).wait_recv()
-    modal(1 - core)
+        modal(1 - core, q)
 
     @pl.when(has_above)
     def _():

time: 39.3 us -> 39.5 us (level)
  no operation moved by 1% of the time
where the time goes in v8:
time: 39.5 us; the launch traced here: 39.4 us
  Pallas kernels  38.8 us (98%)
  between operations  0.64 us (2%)
    pallas_call x1, Pallas kernels, shards(): pl.pallas_call(kernel, out_shape=(whole, half, half, table, table), in_sp...  37.4 us
    pallas_call x1, Pallas kernels, shards(): pl.pallas_call(finish, out_shape=(whole, whole), in_specs=[close] * 5, ou...  1.41 us

profile of v8, /device:TPU:1, one launch (start us, length us, event | category | flops | bytes accessed | tf_op | source)
XLA Modules:
  0.0 39.4 jit_solution(15610345843114866276)
XLA Ops:
  0.6 37.4 %shard_map.86 = (f32[4,256,256]{2,1,0:T(8,128)S(1)}, bf16[4,256,256]{2,1,0:T(8,128)(2,1)S(1)}, bf16[4,256,256]{2,1,0:T(8,128)(2,1)S(1)}, bf16[256,256]{1,0:T(8,128)(2,1)S(1)}, bf16[256,256]{1,0:T(8,128)(2,1)S(1)}) custom-call(f32[4,256,256]{2,1,0:T(8,128)} %frac_in.1, s32[4,256,256]{2,1,0:T(8,128)} %dir_in.1, f32[4,256,256]{2,1,0:T(8,128)} %div_in.1, ...), custom_call_target="tpu_custom_call" | custom-call | tf_op jit(solution)/shard_map/pallas_call | solution.py:583
  38.0 1.4 %shard_map.87 = (f32[4,256,256]{2,1,0:T(8,128)}, f32[4,256,256]{2,1,0:T(8,128)}) custom-call(f32[4,256,256]{2,1,0:T(8,128)S(1)} %get-tuple-element.7.kap, bf16[4,256,256]{2,1,0:T(8,128)(2,1)S(1)} %get-tuple-element.8.high, bf16[4,256,256]{2,1,0:T(8,128)(2,1)S(1)} %get-tuple-element.9.low, bf16[256,256]{1,0:T(8,128)(2,1)S(1)} %get-tuple-element.10.th, ...), custom_call_target="tpu_custom_call" | custom-call | tf_op jit(solution)/shard_map/pallas_call | solution.py:602

commit v9 on v8

--- a/solution.py
+++ b/solution.py
@@ -76,8 +76,8 @@
     kap, inner_high, inner_low, th, tl,
     fx, dirs, divs, ratio, weight,
     axc, axd, axs, ayc, ayd, ays, shi, slo, fhi, flo, spec, part, heights,
-    lus, rc, pu, ru, od, rd, sd, ab,
-    in_sem, fs_sem, fr_sem, c_sem, u_sem, round_sem,
+    lus, rc, rz, pu, ru, od, rd, sd, ab,
+    in_sem, fs_sem, fr_sem, c_sem, z_sem, u_sem, h_sem, round_sem,
 ):
     me = lax.axis_index("gz")
     core = lax.rem(me, 2)
@@ -101,6 +101,7 @@
     nearest = chips_at([(1, 0, 0), (3, 0, 0), (0, 1, 0), (0, 3, 0), (0, 0, 1), (0, 0, 3)])
     y_ring = chips_at([(0, 2, 0), (0, 1, 0), (0, 3, 0)])
     z_ring = chips_at([(2, 0, 0), (1, 0, 0), (3, 0, 0)])
+    x_near = chips_at([(0, 0, 1), (0, 0, 3)])
 
     barrier = pltpu.get_barrier_semaphore()
 
@@ -363,8 +364,6 @@
         late_piece(c)
         if c == 0:
             first_stage((second,))
-        if c == 1:
-            second_stage((second,), slice(None))
 
     def half_rows(half):
         return pl.ds(pl.multiple_of(half * 128, 128), 128)
@@ -381,7 +380,7 @@
         high = r * high + f[0]
         return low, high
 
-    second_stage(late, half_rows(1 - core))
+    second_stage((second,) + late, half_rows(1 - core))
 
     def give(q):
         rows = pl.ds(64 * q, 64)
@@ -396,10 +395,19 @@
             lus[0, rows, :], lus[1, rows, :] = sums(1 - core, i)
         give(q).start()
 
-    second_stage(late, half_rows(core))
+    second_stage((second,) + late, half_rows(core))
     for i in range(4):
         rows = pl.ds(i * ROWS, ROWS)
         rc[core, 0, rows, :], rc[core, 1, rows, :] = sums(core, i)
+
+    share = pltpu.make_async_remote_copy(
+        src_ref=rc.at[0], dst_ref=rz, send_sem=z_sem.at[0], recv_sem=z_sem.at[1],
+        device_id=(sibling,), device_id_type=MESH,
+    )
+
+    @pl.when(core == 0)
+    def _():
+        share.start()
 
     def power4(x):
         x = x * x
@@ -426,20 +434,29 @@
         give(q).wait_recv()
         lax.fori_loop(8 * q, 8 * q + 8, cut, 0, unroll=True)
 
-    def send_part(other, level, source_ref, target_ref):
+    def send_up(other):
         return pltpu.make_async_remote_copy(
-            src_ref=source_ref.at[other], dst_ref=target_ref.at[chip], send_sem=u_sem.at[level, 0],
-            recv_sem=u_sem.at[level, 1], device_id=(2 * other + core,), device_id_type=MESH,
+            src_ref=pu.at[other], dst_ref=ru.at[chip], send_sem=u_sem.at[0], recv_sem=u_sem.at[1],
+            device_id=(2 * other + core,), device_id_type=MESH,
         )
 
-    def wait_parts(level, way):
-        span = pl.ds(0, CHIPS - 1)
-        pltpu.make_async_copy(pu.at[span], ru.at[span], u_sem.at[level, way]).wait()
+    def send_down(other):
+        return pltpu.make_async_remote_copy(
+            src_ref=od.at[other], dst_ref=rd.at[core, chip], send_sem=u_sem.at[2], recv_sem=u_sem.at[3 + core],
+            device_id=(2 * other + 1,), device_id_type=MESH,
+        )
+
+    def wait_parts(sem, count=CHIPS - 1):
+        span = pl.ds(0, count)
+        pltpu.make_async_copy(pu.at[span], ru.at[span], u_sem.at[sem]).wait()
 
     pl.semaphore_wait(round_sem.at[2], len(z_ring))
+    hail(3, x_near)
     for other in others:
-        send_part(other, 0, pu, ru).start()
+        send_up(other).start()
     ru[chip] = pu[chip]
+    wait_parts(1)
+
     tile_row = lax.div(chip, 4)
     tile_lane = lax.rem(lax.div(chip, 2), 2)
     tile_half = lax.rem(chip, 2)
@@ -452,9 +469,6 @@
     r8 = power4(rt * rt)
     r64 = power4(r8 * r8)
     r513 = power4(r64 * r64) * rt
-    settle = 1.0 / (1.0 - r513 * r513)
-    wait_parts(0, 1)
-
     merged = [jnp.where(first_half, ru[j], ru[CHIPS - 1 - j]) for j in range(CHIPS)]
     blocks = []
     for b in range(8):
@@ -465,7 +479,7 @@
     ends = blocks[0]
     for b in range(1, 8):
         ends = r64 * ends + blocks[b]
-    walls = (swap(ends) - r513 * ends) * settle
+    walls = (swap(ends) - r513 * ends) / (1.0 - r513 * r513)
     starts = [-(rt * walls)]
     for b in range(7):
         starts.append(r64 * starts[b] + blocks[b])
@@ -477,61 +491,76 @@
     for j in range(CHIPS):
         od[j] = jnp.where(first_half, sweep[j], sweep[CHIPS - 1 - j])
 
+    pl.semaphore_wait(round_sem.at[3], len(x_near))
     for other in others:
-        send_part(other, 1, od, rd).start()
-    rd[chip] = od[chip]
-    wait_parts(1, 1)
-
-    def spread(i, carry):
-        rows = pl.ds(pl.multiple_of(i * 8, 8), 8)
-        rho = power4(ratio[pl.ds(pl.multiple_of(core * 128 + i * 8, 8), 8), :])
-        tiles = [rd[i * 4 + k] for k in range(4)]
-        a = jnp.concatenate([jnp.where(first_half, tiles[k], swap(tiles[k + 1])) for k in (0, 2)], axis=1)
-        b = jnp.concatenate([jnp.where(first_half, swap(tiles[k]), tiles[k + 1]) for k in (0, 2)], axis=1)
-        a_far = rho * a + rc[0, 0, rows, :]
-        b_far = rho * b + rc[1, 1, rows, :]
-        even = core == 0
-        ab[core, 0, rows, :] = jnp.where(even, a, a_far)
-        ab[core, 1, rows, :] = jnp.where(even, b_far, b)
-        sd[0, rows, :] = jnp.where(even, a_far, a)
-        sd[1, rows, :] = jnp.where(even, b, b_far)
-        return carry
-
-    def hand(q):
-        rows = pl.ds(64 * q, 64)
+        send_down(other).start()
+
+    @pl.when(core == 0)
+    def _():
+        send_down(chip).start()
+
+    def spread(half):
+        even_low, odd_high = (rz.at[0], lus.at[1]) if half == 0 else (rc.at[0, 0], rc.at[1, 1])
+
+        def body(i, carry):
+            rows = pl.ds(pl.multiple_of(i * 8, 8), 8)
+            rho = power4(ratio[pl.ds(pl.multiple_of(half * 128 + i * 8, 8), 8), :])
+            tiles = [rd[half, i * 4 + k] for k in range(4)]
+            a = jnp.concatenate([jnp.where(first_half, tiles[k], swap(tiles[k + 1])) for k in (0, 2)], axis=1)
+            b = jnp.concatenate([jnp.where(first_half, swap(tiles[k]), tiles[k + 1]) for k in (0, 2)], axis=1)
+            sd[half, 0, rows, :] = a
+            sd[half, 1, rows, :] = rho * b + odd_high[rows, :]
+            ab[half, 0, rows, :] = rho * a + even_low[rows, :]
+            ab[half, 1, rows, :] = b
+            return carry
+
+        lax.fori_loop(0, 16, body, 0, unroll=True)
+
+    def hand(half):
         return pltpu.make_async_remote_copy(
-            src_ref=sd.at[:, rows], dst_ref=ab.at[core, :, rows], send_sem=c_sem.at[2, q], recv_sem=c_sem.at[3, q],
+            src_ref=sd.at[half], dst_ref=ab.at[half], send_sem=h_sem.at[0, half], recv_sem=h_sem.at[1, half],
             device_id=(sibling,), device_id_type=MESH,
         )
 
-    for q in range(2):
-        lax.fori_loop(8 * q, 8 * q + 8, spread, 0, unroll=True)
-        hand(q).start()
-
-    def modal(half, q):
-        local = pl.ds(64 * q, 64)
-        rows = pl.ds(pl.multiple_of(half * 128 + 64 * q, 64), 64)
+    def modal(half):
+        rows = pl.ds(128 * half, 128)
         r = ratio[rows, :]
         w = weight[rows, :]
         f = [spec[t, rows, :] for t in range(SLAB + 2)]
-        rising = [r * f[0] + ab[half, 0, local, :] + f[1]]
+        rising = [r * f[0] + ab[half, 0] + f[1]]
         for t in range(1, SLAB):
             rising.append(r * rising[t - 1] + f[t + 1])
-        falling = ab[half, 1, local, :] + r * f[SLAB + 1]
+        falling = ab[half, 1] + r * f[SLAB + 1]
         values = [None] * SLAB
         for t in range(SLAB - 1, -1, -1):
             values[t] = w * (rising[t] + falling)
             falling = r * (falling + f[t + 1])
         high, low = split(mm3(*split(jnp.concatenate(values, axis=0)), th[...], tl[...]))
         for t in range(SLAB):
-            inner_high[t, rows, :] = high[64 * t : 64 * t + 64]
-            inner_low[t, rows, :] = low[64 * t : 64 * t + 64]
-
-    for q in range(2):
-        modal(core, q)
-    for q in range(2):
-        hand(q).wait_recv()
-        modal(1 - core, q)
+            inner_high[t, rows, :] = high[128 * t : 128 * t + 128]
+            inner_low[t, rows, :] = low[128 * t : 128 * t + 128]
+
+    @pl.when(core == 1)
+    def _():
+        rd[1, chip] = od[chip]
+        for half in (1, 0):
+            wait_parts(3 + half, CHIPS - half)
+            if half == 0:
+                share.wait_recv()
+            spread(half)
+            hand(half).start()
+            modal(half)
+        for half in (1, 0):
+            hand(half).wait_send()
+        wait_parts(2, CHIPS - 1)
+
+    @pl.when(core == 0)
+    def _():
+        for half in (1, 0):
+            hand(half).wait_recv()
+            modal(half)
+        share.wait_send()
+        wait_parts(2, CHIPS)
 
     @pl.when(has_above)
     def _():
@@ -545,9 +574,7 @@
 
     for q in range(2):
         give(q).wait_send()
-        hand(q).wait_send()
-    wait_parts(0, 0)
-    wait_parts(1, 0)
+    wait_parts(0)
 
 
 def finish(kap, high, low, th, tl, kap_out, pre_out, pre, sem):
@@ -591,11 +618,11 @@
             six, six, six, six, six, six,
             six_half, six_half, six_half, six_half, six,
             vm((2,) + plane, F32), vm((1,) + plane, F32),
-            vm((2, 128, SIZE), F32), vm((2, 2, 128, SIZE), F32),
+            vm((2, 128, SIZE), F32), vm((2, 2, 128, SIZE), F32), vm((2, 128, SIZE), F32),
             vm((CHIPS, 8, 128), F32), vm((CHIPS, 8, 128), F32),
-            vm((CHIPS, 8, 128), F32), vm((CHIPS, 8, 128), F32),
-            vm((2, 128, SIZE), F32), vm((2, 2, 128, SIZE), F32),
-            dma((7,)), dma((2, 5)), dma((2, 5)), dma((4, 2)), dma((2, 2)), pltpu.SemaphoreType.REGULAR((3,)),
+            vm((CHIPS, 8, 128), F32), vm((2, CHIPS, 8, 128), F32),
+            vm((2, 2, 128, SIZE), F32), vm((2, 2, 128, SIZE), F32),
+            dma((7,)), dma((2, 5)), dma((2, 5)), dma((2, 2)), dma((2,)), dma((5,)), dma((2, 2)), pltpu.SemaphoreType.REGULAR((4,)),
         ],
         compiler_params=pltpu.CompilerParams(collective_id=0, has_side_effects=True, **params),
     )(*(pltpu.with_memory_space_constraint(value, pltpu.HBM) for value in inputs))

time: 39.5 us -> 38.2 us (0.967)
  Pallas kernels: 38.8 us -> 37.4 us
    pallas_call x1, Pallas kernels: 37.4 us -> 36 us  [shards(): pl.pallas_call(kernel, out_shape=(whole, half, half, table, table), in_sp...]
where the time goes in v9:
time: 38.2 us; the launch traced here: 38.1 us
  Pallas kernels  37.4 us (98%)
  between operations  0.64 us (2%)
    pallas_call x1, Pallas kernels, shards(): pl.pallas_call(kernel, out_shape=(whole, half, half, table, table), in_sp...  36 us
    pallas_call x1, Pallas kernels, shards(): pl.pallas_call(finish, out_shape=(whole, whole), in_specs=[close] * 5, ou...  1.41 us

profile of v9, /device:TPU:1, one launch (start us, length us, event | category | flops | bytes accessed | tf_op | source)
XLA Modules:
  0.0 38.1 jit_solution(6014975336026985886)
XLA Ops:
  0.6 36.0 %shard_map.86 = (f32[4,256,256]{2,1,0:T(8,128)S(1)}, bf16[4,256,256]{2,1,0:T(8,128)(2,1)S(1)}, bf16[4,256,256]{2,1,0:T(8,128)(2,1)S(1)}, bf16[256,256]{1,0:T(8,128)(2,1)S(1)}, bf16[256,256]{1,0:T(8,128)(2,1)S(1)}) custom-call(f32[4,256,256]{2,1,0:T(8,128)} %frac_in.1, s32[4,256,256]{2,1,0:T(8,128)} %dir_in.1, f32[4,256,256]{2,1,0:T(8,128)} %div_in.1, ...), custom_call_target="tpu_custom_call" | custom-call | tf_op jit(solution)/shard_map/pallas_call | solution.py:610
  36.7 1.4 %shard_map.87 = (f32[4,256,256]{2,1,0:T(8,128)}, f32[4,256,256]{2,1,0:T(8,128)}) custom-call(f32[4,256,256]{2,1,0:T(8,128)S(1)} %get-tuple-element.7.kap, bf16[4,256,256]{2,1,0:T(8,128)(2,1)S(1)} %get-tuple-element.8.high, bf16[4,256,256]{2,1,0:T(8,128)(2,1)S(1)} %get-tuple-element.9.low, bf16[256,256]{1,0:T(8,128)(2,1)S(1)} %get-tuple-element.10.th, ...), custom_call_target="tpu_custom_call" | custom-call | tf_op jit(solution)/shard_map/pallas_call | solution.py:629

commit v10 on v9

--- a/solution.py
+++ b/solution.py
@@ -444,6 +444,12 @@
         return pltpu.make_async_remote_copy(
             src_ref=od.at[other], dst_ref=rd.at[core, chip], send_sem=u_sem.at[2], recv_sem=u_sem.at[3 + core],
             device_id=(2 * other + 1,), device_id_type=MESH,
+        )
+
+    def send_across(other):
+        return pltpu.make_async_remote_copy(
+            src_ref=od.at[other], dst_ref=rd.at[0, chip], send_sem=u_sem.at[5], recv_sem=u_sem.at[3],
+            device_id=(2 * other,), device_id_type=MESH,
         )
 
     def wait_parts(sem, count=CHIPS - 1):
@@ -492,14 +498,20 @@
         od[j] = jnp.where(first_half, sweep[j], sweep[CHIPS - 1 - j])
 
     pl.semaphore_wait(round_sem.at[3], len(x_near))
-    for other in others:
-        send_down(other).start()
 
     @pl.when(core == 0)
     def _():
+        for other in others:
+            send_down(other).start()
+            send_across(other).start()
         send_down(chip).start()
 
-    def spread(half):
+    @pl.when(core == 1)
+    def _():
+        for other in others:
+            send_down(other).start()
+
+    def spread(half, even=False):
         even_low, odd_high = (rz.at[0], lus.at[1]) if half == 0 else (rc.at[0, 0], rc.at[1, 1])
 
         def body(i, carry):
@@ -508,8 +520,13 @@
             tiles = [rd[half, i * 4 + k] for k in range(4)]
             a = jnp.concatenate([jnp.where(first_half, tiles[k], swap(tiles[k + 1])) for k in (0, 2)], axis=1)
             b = jnp.concatenate([jnp.where(first_half, swap(tiles[k]), tiles[k + 1]) for k in (0, 2)], axis=1)
-            sd[half, 0, rows, :] = a
-            sd[half, 1, rows, :] = rho * b + odd_high[rows, :]
+            if even:
+                ab[half, 0, rows, :] = a
+                ab[half, 1, rows, :] = rho * b + rc[1, 1, rows, :]
+                return carry
+            if half == 1:
+                sd[half, 0, rows, :] = a
+                sd[half, 1, rows, :] = rho * b + odd_high[rows, :]
             ab[half, 0, rows, :] = rho * a + even_low[rows, :]
             ab[half, 1, rows, :] = b
             return carry
@@ -548,19 +565,23 @@
             if half == 0:
                 share.wait_recv()
             spread(half)
-            hand(half).start()
+            if half == 1:
+                hand(half).start()
             modal(half)
-        for half in (1, 0):
-            hand(half).wait_send()
+        hand(1).wait_send()
         wait_parts(2, CHIPS - 1)
 
     @pl.when(core == 0)
     def _():
-        for half in (1, 0):
-            hand(half).wait_recv()
-            modal(half)
+        rd[0, chip] = od[chip]
+        hand(1).wait_recv()
+        modal(1)
+        wait_parts(3)
+        spread(0, True)
+        modal(0)
         share.wait_send()
         wait_parts(2, CHIPS)
+        wait_parts(5)
 
     @pl.when(has_above)
     def _():
@@ -622,7 +643,7 @@
             vm((CHIPS, 8, 128), F32), vm((CHIPS, 8, 128), F32),
             vm((CHIPS, 8, 128), F32), vm((2, CHIPS, 8, 128), F32),
             vm((2, 2, 128, SIZE), F32), vm((2, 2, 128, SIZE), F32),
-            dma((7,)), dma((2, 5)), dma((2, 5)), dma((2, 2)), dma((2,)), dma((5,)), dma((2, 2)), pltpu.SemaphoreType.REGULAR((4,)),
+            dma((7,)), dma((2, 5)), dma((2, 5)), dma((2, 2)), dma((2,)), dma((6,)), dma((2, 2)), pltpu.SemaphoreType.REGULAR((4,)),
         ],
         compiler_params=pltpu.CompilerParams(collective_id=0, has_side_effects=True, **params),
     )(*(pltpu.with_memory_space_constraint(value, pltpu.HBM) for value in inputs))

time: 38.2 us -> 38.5 us (level)
  no operation moved by 1% of the time
where the time goes in v10:
time: 38.5 us; the launch traced here: 38.4 us
  Pallas kernels  37.7 us (98%)
  between operations  0.64 us (2%)
    pallas_call x1, Pallas kernels, shards(): pl.pallas_call(kernel, out_shape=(whole, half, half, table, table), in_sp...  36.3 us
    pallas_call x1, Pallas kernels, shards(): pl.pallas_call(finish, out_shape=(whole, whole), in_specs=[close] * 5, ou...  1.41 us

profile of v10, /device:TPU:1, one launch (start us, length us, event | category | flops | bytes accessed | tf_op | source)
XLA Modules:
  0.0 38.4 jit_solution(7628122166825306752)
XLA Ops:
  0.6 36.3 %shard_map.86 = (f32[4,256,256]{2,1,0:T(8,128)S(1)}, bf16[4,256,256]{2,1,0:T(8,128)(2,1)S(1)}, bf16[4,256,256]{2,1,0:T(8,128)(2,1)S(1)}, bf16[256,256]{1,0:T(8,128)(2,1)S(1)}, bf16[256,256]{1,0:T(8,128)(2,1)S(1)}) custom-call(f32[4,256,256]{2,1,0:T(8,128)} %frac_in.1, s32[4,256,256]{2,1,0:T(8,128)} %dir_in.1, f32[4,256,256]{2,1,0:T(8,128)} %div_in.1, ...), custom_call_target="tpu_custom_call" | custom-call | tf_op jit(solution)/shard_map/pallas_call | solution.py:631
  37.0 1.4 %shard_map.87 = (f32[4,256,256]{2,1,0:T(8,128)}, f32[4,256,256]{2,1,0:T(8,128)}) custom-call(f32[4,256,256]{2,1,0:T(8,128)S(1)} %get-tuple-element.7.kap, bf16[4,256,256]{2,1,0:T(8,128)(2,1)S(1)} %get-tuple-element.8.high, bf16[4,256,256]{2,1,0:T(8,128)(2,1)S(1)} %get-tuple-element.9.low, bf16[256,256]{1,0:T(8,128)(2,1)S(1)} %get-tuple-element.10.th, ...), custom_call_target="tpu_custom_call" | custom-call | tf_op jit(solution)/shard_map/pallas_call | solution.py:650
